TPU v7x, 128 devices: a whole 4x4x4 slice. The times are simulated.
128 devices in a mesh: dp: 2 (over core), graph: 64 (over z, x, y).
Axes of the slice: x: 4, y: 4, z: 4, core: 2. Of those that a mesh axis runs over, the one named last changes fastest.
Arguments:
- grid_latent: bfloat16 [2, 131072, 512], P('dp', 'graph'), may hold values from -6 to 6
- mesh_init: bfloat16 [2, 16384, 512], P('dp', 'graph'), may hold values from -6 to 6
- cotangent: bfloat16 [2, 131072, 512], P('dp', 'graph'), may hold values from -6 to 6
- enc_senders: int32 [12, 16384], P(None, 'graph'), may hold values from 0 to 131071, as said below
- enc_counts: int32 [16384], P('graph'), may hold values from 3 to 12, as said below
- dec_senders: int32 [3, 131072], P(None, 'graph'), may hold values from 0 to 16383, as said below
- recv_weight: bfloat16 [512, 512], replicated, may hold values from -0.25 to 0.25
- send_weight: bfloat16 [512, 512], replicated, may hold values from -0.25 to 0.25
- update_weight: bfloat16 [512, 512], replicated, may hold values from -0.25 to 0.25
- norm_gain: bfloat16 [512], replicated, may hold values from 0.099609375 to 1.8984375
- mesh_send_weight: bfloat16 [512, 512], replicated, may hold values from -0.25 to 0.25
- grid_recv_weight: bfloat16 [512, 512], replicated, may hold values from -0.25 to 0.25
- output_weight: bfloat16 [512, 512], replicated, may hold values from -0.25 to 0.25
Outputs:
- grid_grad: bfloat16 [2, 131072, 512], P('dp', 'graph')
- mesh_grad: bfloat16 [2, 16384, 512], P('dp', 'graph')
- recv_grad: float32 [512, 512], replicated
- send_grad: float32 [512, 512], replicated
- update_grad: float32 [512, 512], replicated
- gain_grad: float32 [512], replicated
- msend_grad: float32 [512, 512], replicated
- grecv_grad: float32 [512, 512], replicated
- out_grad: float32 [512, 512], replicated
Inputs may be any that keep to these rules, and one draw needn't show every extreme that they name: For mesh node m of patch p = m // 256 and position q = m % 256, every enc_senders[k, m] lies in [p * 2048 + q * 8 - 256, p * 2048 + (q + 1) * 8 + 256); slots k >= enc_counts[m] are padding. `enc_counts`: mesh nodes of the first and last 64 // 4 patches have 3 * 3 to 12 edges, the others 12 // 4 to 6. For grid node g of band b = g // 2048 and position q = g % 2048, every dec_senders[j, g] lies in [b * 256 + q * 256 // 2048 - 64, b * 256 + q * 256 // 2048 + 64].
All inputs are finite; a program needn't handle non-finite values.
Results may differ from a plain program's by a relative error of at most 0.02.
Values may be sent and summed in bfloat16 or wider, within the bound.
A program may use at most 192 MiB of HBM per device.

v0:
```python
import math

import jax
import jax.numpy as jnp
from jax import lax
from jax.sharding import PartitionSpec as P

KE = 12
GRIM = 256
MRIM = 64


def with_halo(block, sides, width):
    for axis, dim in sides:
        count = lax.axis_size(axis)
        forward = [(i, i + 1) for i in range(count - 1)]
        backward = [(target, source) for source, target in forward]
        low = lax.ppermute(
            lax.slice_in_dim(block, block.shape[dim] - width, None, axis=dim), axis, forward
        )
        high = lax.ppermute(lax.slice_in_dim(block, 0, width, axis=dim), axis, backward)
        block = jnp.concatenate([low, block, high], axis=dim)
    return block


def activation(pre_value):
    gate_sig = jax.nn.sigmoid(pre_value)
    return (pre_value * gate_sig, gate_sig * (1.0 + pre_value * (1.0 - gate_sig)))


def dot_rows(left, right):
    return lax.dot_general(
        left, right, (((0,), (0,)), ((), ())), preferred_element_type=jnp.float32
    )


def dot_cols(left, right):
    return lax.dot_general(
        left, right, (((1,), (1,)), ((), ())), preferred_element_type=jnp.float32
    )


def selector_block(index, number, block, numer, denom, width):
    window_start = number * block * numer // denom
    picked = lax.dynamic_slice_in_dim(index, number * block, block, 1) - window_start
    selector = (picked[..., None] == jnp.arange(width, dtype=jnp.int32)).astype(jnp.bfloat16)
    return (window_start, selector)


def window_take(extended, index, block, numer, denom, width):
    slots, columns = index.shape
    blocks = columns // block

    def one_block(number):
        window_start, selector = selector_block(index, number, block, numer, denom, width)
        window = lax.dynamic_slice_in_dim(extended, window_start, width, 0)
        return jnp.einsum(
            "smw,wd->smd", selector, window, preferred_element_type=jnp.float32
        ).astype(jnp.bfloat16)

    taken = lax.map(one_block, jnp.arange(blocks, dtype=jnp.int32))
    return jnp.transpose(taken, (1, 0, 2, 3)).reshape(slots, columns, extended.shape[1])


def window_add(total_rows, index, values, block, numer, denom, width):
    columns = index.shape[1]
    blocks = columns // block

    def one_block(totals, number):
        window_start, selector = selector_block(index, number, block, numer, denom, width)
        part_values = lax.dynamic_slice_in_dim(values, number * block, block, 1)
        added = jnp.einsum("smw,smd->wd", selector, part_values, preferred_element_type=jnp.float32)
        current = lax.dynamic_slice_in_dim(totals, window_start, width, 0)
        return (lax.dynamic_update_slice_in_dim(totals, current + added, window_start, 0), 0)

    start_totals = jnp.zeros((total_rows, values.shape[2]), jnp.float32)
    totals, unused = lax.scan(one_block, start_totals, jnp.arange(blocks, dtype=jnp.int32))
    return totals


def neighbour_rows(values, depth):
    return with_halo(values, (("graph", 0),), depth)


def return_rims(extended, depth):
    rims = jnp.concatenate([extended[:depth], extended[-depth:]], 0)
    arrived = with_halo(rims, (("graph", 0),), depth)
    owned = extended[depth:-depth]
    owned = owned.at[:depth].add(arrived[:depth])
    return owned.at[-depth:].add(arrived[-depth:])


def slot_forward(gathered, receiver, live_mask):
    enc_pre = gathered.astype(jnp.float32) + receiver.astype(jnp.float32)[None]
    value, slope = activation(enc_pre)
    return (jnp.sum(value * live_mask[..., None], axis=0), slope * live_mask[..., None])


def shards(
    grid_latent,
    mesh_init,
    cotangent,
    enc_senders,
    enc_counts,
    dec_senders,
    recv_weight,
    send_weight,
    update_weight,
    norm_gain,
    mesh_send_weight,
    grid_recv_weight,
    output_weight,
):
    band_index = lax.axis_index("graph")
    grid_in = grid_latent[0]
    mesh_in = mesh_init[0]
    grid_cot = cotangent[0]
    grid_rows = grid_in.shape[0]
    mesh_rows = mesh_in.shape[0]
    ratio_rows = grid_rows // mesh_rows
    enc_block = min(mesh_rows, 128)
    enc_width = enc_block * ratio_rows + 2 * GRIM
    dec_block = min(grid_rows, 512)
    dec_width = dec_block // ratio_rows + 2 * MRIM
    send_proj = jnp.dot(grid_in, send_weight, preferred_element_type=jnp.float32).astype(
        jnp.bfloat16
    )
    send_ext = neighbour_rows(send_proj, GRIM)
    recv_proj = jnp.dot(mesh_in, recv_weight, preferred_element_type=jnp.float32).astype(
        jnp.bfloat16
    )
    local_index = enc_senders - (band_index * grid_rows - GRIM)
    live_mask = (jnp.arange(KE, dtype=jnp.int32)[:, None] < enc_counts[None, :]).astype(jnp.float32)
    agg_total, deriv_all = slot_forward(
        window_take(send_ext, local_index, enc_block, ratio_rows, 1, enc_width),
        recv_proj,
        live_mask,
    )
    aggregate = agg_total.astype(jnp.bfloat16)
    update = jnp.dot(aggregate, update_weight, preferred_element_type=jnp.float32)
    inv_rms = lax.rsqrt(jnp.mean(update * update, axis=-1, keepdims=True) + 1e-06)
    normed = update * inv_rms
    mesh_latent = (mesh_in.astype(jnp.float32) + norm_gain.astype(jnp.float32) * normed).astype(
        jnp.bfloat16
    )
    mesh_proj = jnp.dot(mesh_latent, mesh_send_weight, preferred_element_type=jnp.float32).astype(
        jnp.bfloat16
    )
    mesh_ext = neighbour_rows(mesh_proj, MRIM)
    dec_index = dec_senders - (band_index * mesh_rows - MRIM)
    grid_proj = jnp.dot(grid_in, grid_recv_weight, preferred_element_type=jnp.float32)
    dec_rows = window_take(mesh_ext, dec_index, dec_block, 1, ratio_rows, dec_width)
    dec_pre = dec_rows.astype(jnp.float32) + grid_proj[None]
    dec_value, dec_slope = activation(dec_pre)
    dec_sum = jnp.sum(dec_value, axis=0).astype(jnp.bfloat16)
    out_term = dot_rows(dec_sum, grid_cot)
    sum_cot = dot_cols(grid_cot, output_weight)
    dec_narrow = lax.optimization_barrier((sum_cot[None] * dec_slope).astype(jnp.bfloat16))
    recv_cot = jnp.sum(dec_narrow.astype(jnp.float32), axis=0).astype(jnp.bfloat16)
    mesh_cot_ext = window_add(
        mesh_rows + 2 * MRIM, dec_index, dec_narrow, dec_block, 1, ratio_rows, dec_width
    )
    mesh_cot = return_rims(mesh_cot_ext, MRIM).astype(jnp.bfloat16)
    grecv_term = dot_rows(grid_in, recv_cot)
    msend_term = dot_rows(mesh_latent, mesh_cot)
    latent_cot = dot_cols(mesh_cot, mesh_send_weight)
    gain_term = jnp.sum(latent_cot * normed, axis=0)
    normed_cot = latent_cot * norm_gain.astype(jnp.float32)
    update_cot = (
        (normed_cot - normed * jnp.mean(normed_cot * normed, axis=-1, keepdims=True)) * inv_rms
    ).astype(jnp.bfloat16)
    update_term = dot_rows(aggregate, update_cot)
    agg_cot = dot_cols(update_cot, update_weight)
    enc_cot = (agg_cot[None] * deriv_all).astype(jnp.bfloat16)
    enc_cot = lax.optimization_barrier(enc_cot)
    recv_sum = jnp.sum(enc_cot.astype(jnp.float32), axis=0).astype(jnp.bfloat16)
    send_cot_ext = window_add(
        grid_rows + 2 * GRIM, local_index, enc_cot, enc_block, ratio_rows, 1, enc_width
    )
    send_cot = return_rims(send_cot_ext, GRIM).astype(jnp.bfloat16)
    recv_term = dot_rows(mesh_in, recv_sum)
    send_term = dot_rows(grid_in, send_cot)
    mesh_grad = (latent_cot + dot_cols(recv_sum, recv_weight)).astype(jnp.bfloat16)[None]
    grid_total = (
        grid_cot.astype(jnp.float32)
        + dot_cols(recv_cot, grid_recv_weight)
        + dot_cols(send_cot, send_weight)
    )
    grid_grad = grid_total.astype(jnp.bfloat16)[None]
    summed = lax.psum(
        (recv_term, send_term, update_term, gain_term, msend_term, grecv_term, out_term),
        ("dp", "graph"),
    )
    factor = 1.0 / math.sqrt(grid_rows * lax.axis_size("graph") * lax.axis_size("dp"))
    return (
        grid_grad,
        mesh_grad,
        summed[0] * factor,
        summed[1] * factor,
        summed[2] * factor,
        summed[3] * factor,
        summed[4] * factor,
        summed[5] * factor,
        summed[6] * factor,
    )


def solution(mesh):
    return jax.shard_map(
        shards,
        mesh=mesh,
        in_specs=(
            P("dp", "graph", None),
            P("dp", "graph", None),
            P("dp", "graph", None),
            P(None, "graph"),
            P("graph"),
            P(None, "graph"),
            P(),
            P(),
            P(),
            P(),
            P(),
            P(),
            P(),
        ),
        out_specs=(
            P("dp", "graph", None),
            P("dp", "graph", None),
            P(),
            P(),
            P(),
            P(),
            P(),
            P(),
            P(),
        ),
        check_vma=False,
    )
```

profile of v0, /device:TPU:1, one launch (start us, length us, event | category | flops | bytes accessed | tf_op | source)
XLA Modules:
  0.0 416.9 jit_solution(5319600202520810390)
XLA Ops:
  7.2 1.5 copy-done
  8.8 2.3 convolution_convert_fusion.1
  11.1 1.3 copy-done.11
  13.2 4.8 %collective-permute-start = (bf16[256,512]{1,0:T(8,128)(2,1)}, bf16[256,512]{1,0:T(8,128)(2,1)}, u32[]{:S(2)}, u32[]{:S(2)}) collective-permute-start(bf16[256,512]{1,0:T(8,128)(2,1)} %get-tuple-element.388), channel_id=1, source_target_pairs={{0,1},{1,2},{2,3},{3,4},{4,5},{5,6},{6,7},{7,8},{8,9},{9,10},{10,1... | collective-permute-start | bytes 786440 | tf_op jit(solution)/shard_map/ppermute | solution.py:18
  19.3 3.3 fusion.49
  23.2 5.0 %fusion.54 = f32[2048,512]{1,0:T(8,128)} fusion(bf16[512,512]{1,0:T(8,128)(2,1)} %param.41, bf16[1,2048,512]{2,1,0:T(8,128)(2,1)} %param.31), kind=kOutput, calls=%fused_computation.70 | convolution fusion | flops 1073741824 | bytes 6815744 | tf_op jit(solution)/shard_map/dot_general | solution.py:38
  28.6 3.5 pad_maximum_fusion
  32.1 14.3 %while.52 = (s32[]{:T(128)}, bf16[2,12,128,512]{3,2,1,0:T(8,128)(2,1)}, s32[2]{0:T(128)S(1)}, s32[12,256]{1,0:T(8,128)S(1)}, bf16[2560,512]{1,0:T(8,128)(2,1)}, ...) while((s32[]{:T(128)}, bf16[2,12,128,512]{3,2,1,0:T(8,128)(2,1)}, ...), condition=%wide.region_1.2_spmd, body=%wide.region_0.1_spmd.sunk | while | flops 2419066368 | bytes 3164897 | solution.py:61
  34.0 5.2 %bitcast_dynamic-update-slice_fusion.4 = bf16[2,12,128,512]{3,2,1,0:T(8,128)(2,1)} fusion(bf16[2,12,128,512]{3,2,1,0:T(8,128)(2,1)} %get-tuple-element.539, s32[]{:T(128)} %get-tuple-element.538, bf16[2560,512]{1,0:T(8,128)(2,1)} %get-tuple-element.553, s32[]{:T(128)S(6)} %select_n.84, s32[12,128]{1,0:T(8,128)S(1)} %dynamic-slice_subtract_fusion.8), kind=kOutput, calls=%fused_computation.4.clone.1 | convolution fusion | flops 2419064832 | bytes 3152388 | tf_op jit(solution)/shard_map/while/body/eval_jaxpr/smw,wd->smd/dot_general | solution.py:57
  41.2 5.2 %bitcast_dynamic-update-slice_fusion.4 = bf16[2,12,128,512]{3,2,1,0:T(8,128)(2,1)} fusion(bf16[2,12,128,512]{3,2,1,0:T(8,128)(2,1)} %get-tuple-element.539, s32[]{:T(128)} %get-tuple-element.538, bf16[2560,512]{1,0:T(8,128)(2,1)} %get-tuple-element.553, s32[]{:T(128)S(6)} %select_n.84, s32[12,128]{1,0:T(8,128)S(1)} %dynamic-slice_subtract_fusion.8), kind=kOutput, calls=%fused_computation.4.clone.1 | convolution fusion | flops 2419064832 | bytes 3152388 | tf_op jit(solution)/shard_map/while/body/eval_jaxpr/smw,wd->smd/dot_general | solution.py:57
  46.4 3.6 fusion.43
  50.0 1.5 multiply_reduce_fusion.2
  52.2 4.0 collective-permute-start.2
  56.2 1.5 collective-permute-start.3
  58.6 3.4 copy.23
  62.0 12.5 %while.53 = (s32[]{:T(128)}, bf16[4,3,512,512]{3,2,1,0:T(8,128)(2,1)}, s32[4]{0:T(128)S(1)}, s32[3,2048]{1,0:T(4,128)S(1)}, bf16[384,512]{1,0:T(8,128)(2,1)S(1)}...) while((s32[]{:T(128)}, ...), condition=%wide.region_5.6_spmd, body=%wide.region_4.5_spmd.sunk | while | flops 303072800 | bytes 1790834 | solution.py:61
  63.3 1.8 bitcast_dynamic-update-slice_fusion.5
  66.4 1.8 bitcast_dynamic-update-slice_fusion.5
  69.5 1.8 bitcast_dynamic-update-slice_fusion.5
  72.6 1.9 bitcast_dynamic-update-slice_fusion.5
  74.5 9.1 %convert_bitcast_fusion = f32[3,4,512,512]{3,2,0,1:T(8,128)} fusion(bf16[4,3,512,512]{3,2,1,0:T(8,128)(2,1)} %get-tuple-element.326), kind=kLoop, calls=%fused_computation.35 | loop fusion | flops 3145728 | bytes 18874368 | tf_op jit(solution)/shard_map/convert_element_type | solution.py:153
  83.6 10.8 %copy.22 = f32[3,4,512,512]{3,2,1,0:T(8,128)} copy(f32[3,4,512,512]{3,2,0,1:T(8,128)} %convert_bitcast_fusion) | data formatting | bytes 25165824 | tf_op jit(solution)/shard_map/convert_element_type | solution.py:153
  94.3 11.2 %multiply_convert_fusion = bf16[3,2048,512]{2,1,0:T(8,128)(2,1)} fusion(f32[3,4,512,512]{3,2,1,0:T(8,128)} %copy.22, f32[2048,512]{1,0:T(8,128)S(1)} %copy-done.1, f32[2048,512]{1,0:T(8,128)} %fusion.54), kind=kLoop, calls=%fused_computation.43 | loop fusion | flops 31457280 | bytes 27262976 | tf_op jit(solution)/shard_map/convert_element_type | solution.py:158
  106.1 19.9 %while.54 = (s32[]{:T(128)}, f32[384,512]{1,0:T(8,128)S(1)}, s32[4]{0:T(128)}, s32[3,2048]{1,0:T(4,128)}, bf16[3,2048,512]{2,1,0:T(8,128)(2,1)}, /*index=5*/s32[...) while((s32[]{:T(128)}, f32[384,512]{1,0:T(8,128)S(1)}, ...), condition=%wide.region_8.9_spmd, body=%wide.region_7.8_spmd.sunk | while | flops 302384672 | bytes 3164538 | solution.py:77
  108.7 1.9 fusion.115
  113.7 1.9 fusion.115
  118.7 1.9 fusion.115
  123.6 1.9 fusion.115
  126.7 4.0 collective-permute-start.4
  130.7 1.5 collective-permute-start.5
  132.2 5.8 %reduce_sum.71 = bf16[2048,512]{1,0:T(8,128)(2,1)} reduce(bf16[3,2048,512]{2,1,0:T(8,128)(2,1)} %get-tuple-element.683, bf16[]{:T(256)} %constant.344.clone.1), dimensions={0}, to_apply=%region_6.7 | reduce | flops 2097152 | bytes 8388610 | tf_op jit(solution)/shard_map/reduce_sum | solution.py:159
  138.0 4.0 fusion.59
  142.0 6.2 %fusion.35 = bf16[4,512,512]{2,1,0:T(8,128)(2,1)S(1)} fusion(bf16[4,3,512,512]{3,2,1,0:T(8,128)(2,1)} %get-tuple-element.326, f32[4,512,512]{2,1,0:T(8,128)S(1)} %bitcast.160), kind=kLoop, calls=%fused_computation.44 | loop fusion | flops 20971520 | bytes 12582912 | tf_op jit(solution)/shard_map/reduce_sum | solution.py:155
  148.3 2.3 fusion.52
  152.4 4.1 multiply_convert_fusion.1
  156.5 3.0 broadcast_in_dim.36
  159.5 15.6 %while.55 = (s32[]{:T(128)}, f32[2560,512]{1,0:T(8,128)}, s32[2]{0:T(128)S(1)}, s32[12,256]{1,0:T(8,128)S(1)}, bf16[12,256,512]{2,1,0:T(8,128)(2,1)}, /*index=5*...) while((s32[]{:T(128)}, f32[2560,512]{1,0:T(8,128)}, ...), condition=%wide.region_11.12_spmd, body=%wide.region_10.11_spmd.sunk | while | flops 2419066368 | bytes 7882981 | solution.py:77
  161.4 5.9 %fusion.117 = f32[2560,512]{1,0:T(8,128)} fusion(f32[2560,512]{1,0:T(8,128)} %get-tuple-element.650, s32[]{:T(128)S(6)} %select_n.92, s32[12,128]{1,0:T(8,128)S(1)} %dynamic-slice_subtract_fusion.11, bf16[12,256,512]{2,1,0:T(8,128)(2,1)} %get-tuple-element.664, s32[]{:T(128)S(6)} %select_n.93), kind=kOutput, calls=%fused_computation.30.clone.1 | convolution fusion | flops 2419064832 | bytes 7870472 | tf_op jit(solution)/shard_map/while/body/eval_jaxpr/smw,smd->wd/dot_general | solution.py:72
  169.2 5.9 %fusion.117 = f32[2560,512]{1,0:T(8,128)} fusion(f32[2560,512]{1,0:T(8,128)} %get-tuple-element.650, s32[]{:T(128)S(6)} %select_n.92, s32[12,128]{1,0:T(8,128)S(1)} %dynamic-slice_subtract_fusion.11, bf16[12,256,512]{2,1,0:T(8,128)(2,1)} %get-tuple-element.664, s32[]{:T(128)S(6)} %select_n.93), kind=kOutput, calls=%fused_computation.30.clone.1 | convolution fusion | flops 2419064832 | bytes 7870472 | tf_op jit(solution)/shard_map/while/body/eval_jaxpr/smw,smd->wd/dot_general | solution.py:72
  175.1 4.7 %slice.117 = f32[2048,512]{1,0:T(8,128)} slice(f32[2560,512]{1,0:T(8,128)} %get-tuple-element.328), slice={[256:2304], [0:512]} | slice | bytes 8388608 | tf_op jit(solution)/shard_map/slice | solution.py:88
  179.8 2.3 fusion.77
  182.1 1.3 fusion.71
  183.4 2.4 reduce_sum.73
  185.8 4.0 collective-permute-start.6
  189.9 1.6 collective-permute-start.7
  191.4 2.3 fusion.83
  195.0 4.0 collective-permute-done.6
  199.0 1.9 add_dynamic-update-slice_fusion
  200.9 2.4 collective-permute-done.7
  203.3 1.9 fusion.67
  205.3 4.4 %fusion.56 = f32[512,512]{0,1:T(8,128)} fusion(bf16[1,2048,512]{2,1,0:T(8,128)(2,1)S(1)} %copy-done, f32[2048,512]{1,0:T(8,128)} %fusion.67), kind=kOutput, calls=%fused_computation.73 | convolution fusion | flops 1074790400 | bytes 7340032 | tf_op jit(solution)/shard_map/dot_general | solution.py:32
  210.7 4.8 %fusion.81 = f32[2048,512]{1,0:T(8,128)} fusion(bf16[2048,512]{1,0:T(8,128)(2,1)} %reduce_sum.71, bf16[512,512]{1,0:T(8,128)(2,1)S(1)} %copy-done.17), kind=kOutput, calls=%fused_computation.120 | convolution fusion | flops 1073741824 | bytes 6815744 | tf_op jit(solution)/shard_map/dot_general | solution.py:38
  215.6 84.1 %psum.52 = f32[512]{0:T(512)S(1)} all-reduce(f32[512]{0:T(512)S(1)} %copy-done.30), channel_id=1, replica_groups=mesh['dp'=2,'graph'=64] {'dp','graph'}, use_global_device_ids=true, to_apply=%region_17.18 | all-reduce | flops 512 | bytes 4096 | tf_op jit(solution)/shard_map/psum | solution.py:190
  299.7 2.1 fusion.64
  302.4 6.9 %fusion.44 = bf16[1,2048,512]{2,1,0:T(8,128)(2,1)} fusion(bf16[512,512]{1,0:T(8,128)(2,1)} %param.36, f32[2048,512]{1,0:T(8,128)} %fusion.81, bf16[1,2048,512]{2,1,0:T(8,128)(2,1)} %param.31, f32[2048,512]{1,0:T(8,128)} %fusion.67), kind=kOutput, calls=%fused_computation.59 | convolution fusion | flops 1078984704 | bytes 13107200 | tf_op jit(solution)/shard_map/dot_general | solution.py:38
  309.3 81.0 %all-reduce.3.cloned.1.call-done = (f32[512,512]{0,1:T(8,128)}, f32[512,512]{0,1:T(8,128)}, f32[512,512]{0,1:T(8,128)}, f32[512,512]{0,1:T(8,128)}, f32[512,512]{0,1:T(8,128)}, /*index=5*/f32[512,512]{0,1:T(8,128)}) async-done(((f32[512,512]{0,1:T(8,128)}, f32[512,512]{0,1:T(8,128)}, f32[512,512]{0,1:T(8,128)}, f32[512,512]{0,1:T(8,128)}, f32[512,512]{0,1:T(8,128)}, /*index=5*/f32[512,512]{0,1:T(8,128)}), ...) | async-done | bytes 6291472 | tf_op jit(solution)/shard_map/psum | solution.py:190
  390.3 2.7 broadcast_multiply_fusion
  393.0 2.5 copy.31
  396.9 2.7 broadcast_multiply_fusion.2
  399.6 2.5 copy.29
  402.1 1.3 copy.30
  403.4 2.7 broadcast_multiply_fusion.4
  406.2 2.5 copy.27
  408.7 1.3 copy.28
  (137 shorter events, 26.2 us)
Async XLA Ops:
  7.2 1.6 copy-start
  7.2 12.1 %copy-start.16 = (bf16[512,512]{1,0:T(8,128)(2,1)S(1)}, bf16[512,512]{1,0:T(8,128)(2,1)}, u32[]{:S(2)}) copy-start(bf16[512,512]{1,0:T(8,128)(2,1)} %param.40) | copy-start | bytes 1572868
  7.2 383.1 %all-reduce.3.cloned.1.call-start = ((), (), s32[]{:S(2)}) async-start(), calls=%async_computation | async-start | bytes 12582912 | tf_op jit(solution)/shard_map/psum | solution.py:190
  11.1 1.3 copy-start.11
  13.2 15.4 %collective-permute-start = (bf16[256,512]{1,0:T(8,128)(2,1)}, bf16[256,512]{1,0:T(8,128)(2,1)}, u32[]{:S(2)}, u32[]{:S(2)}) collective-permute-start(bf16[256,512]{1,0:T(8,128)(2,1)} %get-tuple-element.388), channel_id=1, source_target_pairs={{0,1},{1,2},{2,3},{3,4},{4,5},{5,6},{6,7},{7,8},{8,9},{9,10},{10,1... | collective-permute-start | bytes 786440 | tf_op jit(solution)/shard_map/ppermute | solution.py:18
  18.0 10.6 %collective-permute-start.1 = (bf16[256,512]{1,0:T(8,128)(2,1)}, bf16[256,512]{1,0:T(8,128)(2,1)}, u32[]{:S(2)}, u32[]{:S(2)}) collective-permute-start(bf16[256,512]{1,0:T(8,128)(2,1)} %get-tuple-element.389), channel_id=1, source_target_pairs={{1,0},{2,1},{3,2},{4,3},{5,4},{6,5},{7,6},{8,7},{9,8},{10,9},{11,1... | collective-permute-start | bytes 786440 | tf_op jit(solution)/shard_map/ppermute | solution.py:21
  19.3 3.3 copy-start.31
  19.3 3.9 copy-start.29
  19.3 3.9 copy-start.26
  23.2 5.0 %copy-start.32 = (bf16[512]{0:T(512)(128)(2,1)S(1)}, bf16[512]{0:T(512)(128)(2,1)}, u32[]{:S(2)}) copy-start(bf16[512]{0:T(512)(128)(2,1)} %param.38) | copy-start | bytes 3076
  23.2 5.0 %copy-start.12 = (bf16[1,256,512]{2,1,0:T(8,128)(2,1)S(1)}, bf16[1,256,512]{2,1,0:T(8,128)(2,1)}, u32[]{:S(2)}) copy-start(bf16[1,256,512]{2,1,0:T(8,128)(2,1)} %param.30) | copy-start | bytes 786436
  23.2 5.0 %copy-start.20 = (bf16[512,512]{1,0:T(8,128)(2,1)S(1)}, bf16[512,512]{1,0:T(8,128)(2,1)}, u32[]{:S(2)}) copy-start(bf16[512,512]{1,0:T(8,128)(2,1)} %param.35) | copy-start | bytes 1572868
  28.3 23.3 %copy-start.24 = (f32[512]{0:T(512)}, f32[512]{0:T(512)S(1)}, u32[]{:S(2)}) copy-start(f32[512]{0:T(512)S(1)} %convert_element_type.122) | copy-start | bytes 6148
  28.6 17.8 %copy-start.9 = (f32[256,512]{1,0:T(8,128)}, f32[256,512]{1,0:T(8,128)S(1)}, u32[]{:S(2)}) copy-start(f32[256,512]{1,0:T(8,128)S(1)} %fusion.63) | copy-start | bytes 1572868
  46.4 5.3 %copy-start.18 = (bf16[512,512]{1,0:T(8,128)(2,1)S(1)}, bf16[512,512]{1,0:T(8,128)(2,1)}, u32[]{:S(2)}) copy-start(bf16[512,512]{1,0:T(8,128)(2,1)} %param.39) | copy-start | bytes 1572868
  46.4 11.3 %copy-start.4 = (bf16[2,12,128,512]{3,2,1,0:T(8,128)(2,1)S(1)}, bf16[2,12,128,512]{3,2,1,0:T(8,128)(2,1)}, u32[]{:S(2)}) copy-start(bf16[2,12,128,512]{3,2,1,0:T(8,128)(2,1)} %get-tuple-element.325) | copy-start | bytes 9437188
  50.0 8.6 %copy-start.15 = (bf16[2,128,512]{2,1,0:T(8,128)(2,1)}, bf16[2,128,512]{2,1,0:T(8,128)(2,1)S(1)}, u32[]{:S(2)}) copy-start(bf16[2,128,512]{2,1,0:T(8,128)(2,1)S(1)} %fusion.43) | copy-start | bytes 786436
  51.5 4.7 %copy-start.5 = (f32[256,512]{1,0:T(8,128)}, f32[256,512]{1,0:T(8,128)S(1)}, u32[]{:S(2)}) copy-start(f32[256,512]{1,0:T(8,128)S(1)} %get-tuple-element.395) | copy-start | bytes 1572868
  51.5 0.7 copy-start.27
  51.7 4.5 %copy-start.13 = (bf16[256,512]{1,0:T(8,128)(2,1)}, bf16[256,512]{1,0:T(8,128)(2,1)S(1)}, u32[]{:S(2)}) copy-start(bf16[256,512]{1,0:T(8,128)(2,1)S(1)} %add_convert_fusion.1) | copy-start | bytes 786436
  52.2 9.8 %collective-permute-start.2 = (bf16[64,512]{1,0:T(8,128)(2,1)S(1)}, bf16[64,512]{1,0:T(8,128)(2,1)S(1)}, u32[]{:S(2)}, u32[]{:S(2)}) collective-permute-start(bf16[64,512]{1,0:T(8,128)(2,1)S(1)} %get-tuple-element.392), channel_id=1, source_target_pairs={{0,1},{1,2},{2,3},{3,4},{4,5},{5,6},{6,7},{7,8},{8,9},{9,10},{10,1... | collective-permute-start | bytes 196616 | tf_op jit(solution)/shard_map/ppermute | solution.py:18
  56.2 5.7 %collective-permute-start.3 = (bf16[64,512]{1,0:T(8,128)(2,1)S(1)}, bf16[64,512]{1,0:T(8,128)(2,1)S(1)}, u32[]{:S(2)}, u32[]{:S(2)}) collective-permute-start(bf16[64,512]{1,0:T(8,128)(2,1)S(1)} %get-tuple-element.393), channel_id=1, source_target_pairs={{1,0},{2,1},{3,2},{4,3},{5,4},{6,5},{7,6},{8,7},{9,8},{10,9},{11,1... | collective-permute-start | bytes 196616 | tf_op jit(solution)/shard_map/ppermute | solution.py:21
  74.5 9.1 %copy-start.22 = (s32[3,2048]{1,0:T(4,128)}, s32[3,2048]{1,0:T(4,128)S(1)}, u32[]{:S(2)}) copy-start(s32[3,2048]{1,0:T(4,128)S(1)} %get-tuple-element.704) | copy-start | bytes 73732
  83.5 10.8 %copy-start.1 = (f32[2048,512]{1,0:T(8,128)S(1)}, f32[2048,512]{1,0:T(8,128)}, u32[]{:S(2)}) copy-start(f32[2048,512]{1,0:T(8,128)} %fusion.49) | copy-start | bytes 12582916
  126.7 23.9 %collective-permute-start.4 = (f32[64,512]{1,0:T(8,128)}, f32[64,512]{1,0:T(8,128)S(1)}, u32[]{:S(2)}, u32[]{:S(2)}) collective-permute-start(f32[64,512]{1,0:T(8,128)} %get-tuple-element.391), channel_id=1, source_target_pairs={{0,1},{1,2},{2,3},{3,4},{4,5},{5,6},{6,7},{7,8},{8,9},{9,10},{10,1... | collective-permute-start | bytes 393224 | tf_op jit(solution)/shard_map/ppermute | solution.py:18
  130.7 19.9 %collective-permute-start.5 = (f32[64,512]{1,0:T(8,128)S(1)}, f32[64,512]{1,0:T(8,128)S(1)}, u32[]{:S(2)}, u32[]{:S(2)}) collective-permute-start(f32[64,512]{1,0:T(8,128)S(1)} %get-tuple-element.390), channel_id=1, source_target_pairs={{1,0},{2,1},{3,2},{4,3},{5,4},{6,5},{7,6},{8,7},{9,8},{10,9},{11,1... | collective-permute-start | bytes 393224 | tf_op jit(solution)/shard_map/ppermute | solution.py:21
  138.0 4.0 copy-start.2
  142.0 6.2 %copy-start.3 = (bf16[1,2048,512]{2,1,0:T(8,128)(2,1)S(1)}, bf16[1,2048,512]{2,1,0:T(8,128)(2,1)}, u32[]{:S(2)}) copy-start(bf16[1,2048,512]{2,1,0:T(8,128)(2,1)} %param.31) | copy-start | bytes 6291460
  148.2 4.2 slice-start
  148.2 2.5 copy-start.6
  148.2 2.5 copy-start.19
  148.3 2.5 copy-start.25
  148.3 2.5 copy-start.28
  148.3 4.1 slice-start.1
  150.6 1.5 copy-start.21
  150.6 1.8 copy-start.10
  150.6 1.8 copy-start.23
  150.7 1.1 copy-start.7
  175.1 7.0 %copy-start.8 = (f32[256,512]{1,0:T(8,128)S(1)}, f32[256,512]{1,0:T(8,128)}, u32[]{:S(2)}) copy-start(f32[256,512]{1,0:T(8,128)} %copy-done.7) | copy-start | bytes 1572868
  175.1 7.0 %copy-start.14 = (bf16[256,512]{1,0:T(8,128)(2,1)S(1)}, bf16[256,512]{1,0:T(8,128)(2,1)}, u32[]{:S(2)}) copy-start(bf16[256,512]{1,0:T(8,128)(2,1)} %copy-done.13) | copy-start | bytes 786436
  185.8 13.2 %collective-permute-start.6 = (f32[256,512]{1,0:T(8,128)}, f32[256,512]{1,0:T(8,128)S(1)}, u32[]{:S(2)}, u32[]{:S(2)}) collective-permute-start(f32[256,512]{1,0:T(8,128)} %get-tuple-element.387), channel_id=1, source_target_pairs={{0,1},{1,2},{2,3},{3,4},{4,5},{5,6},{6,7},{7,8},{8,9},{9,10},{10,1... | collective-permute-start | bytes 1572872 | tf_op jit(solution)/shard_map/ppermute | solution.py:18
  189.9 13.5 %collective-permute-start.7 = (f32[256,512]{1,0:T(8,128)}, f32[256,512]{1,0:T(8,128)S(1)}, u32[]{:S(2)}, u32[]{:S(2)}) collective-permute-start(f32[256,512]{1,0:T(8,128)} %get-tuple-element.386), channel_id=1, source_target_pairs={{1,0},{2,1},{3,2},{4,3},{5,4},{6,5},{7,6},{8,7},{9,8},{10,9},{11,1... | collective-permute-start | bytes 1572872 | tf_op jit(solution)/shard_map/ppermute | solution.py:21
  209.7 1.0 copy-start.17
  210.7 4.9 %copy-start.30 = (f32[512]{0:T(512)S(1)}, f32[512]{0:T(512)}, u32[]{:S(2)}) copy-start(f32[512]{0:T(512)} %get-tuple-element.338) | copy-start | bytes 6148
Sparse Core Ops, SparseCore 0:
  209.8 180.3 all-reduce.2
where the time goes:
time: 419 us; the launch traced here: 417 us
  waiting for transfers between devices  87.4 us (21%)
  blocking collectives  84.1 us (20%)
  matrix products  80.4 us (19%)
  other arithmetic  63.2 us (15%)
  local copies, waits for them, and re-layouts  53.6 us (13%)
  starting transfers between devices  22.6 us (5%)
  between operations  14.7 us (4%)
  loops' own time  10.9 us (3%)
    psum x1, blocking collectives, shards(): lax.psum((recv_term, send_term, update_term, gain_term, msend_term, grecv...  84.1 us
    psum x1, waiting for transfers between devices, shards(): lax.psum((recv_term, send_term, update_term, gain_term, msend_term, grecv...  81 us
    dot_general x6, matrix products, dot_cols(): lax.dot_general(left, right, (((1,), (1,)), ((), ())), preferred_element_...  20.1 us
    dot_general x6, matrix products, one_block(): jnp.einsum('smw,smd->wd', selector, part_values, preferred_element_type=j...  19.3 us
    dot_general x6, matrix products, one_block(): jnp.einsum('smw,wd->smd', selector, window, preferred_element_type=jnp.fl...  17.8 us
    ppermute x4, starting transfers between devices, with_halo(): lax.ppermute(lax.slice_in_dim(block, block.shape[dim] - width, None, axis...  16.7 us
    unnamed x76, local copies, waits for them, and re-layouts  15.9 us
    dot_general x6, matrix products, dot_rows(): lax.dot_general(left, right, (((0,), (0,)), ((), ())), preferred_element_...  15.6 us
  transfers between devices with their start and end apart: 9, of which 3 were waited for; matrix products, arithmetic and copies ran while one was open for 12% of the time, Pallas kernels for 0%

commit v1 on v0

--- a/solution.py
+++ b/solution.py
@@ -3,6 +3,8 @@
 import jax
 import jax.numpy as jnp
 from jax import lax
+from jax.experimental import pallas as pl
+from jax.experimental.pallas import tpu as pltpu
 from jax.sharding import PartitionSpec as P
 
 KE = 12
@@ -94,6 +96,228 @@
     enc_pre = gathered.astype(jnp.float32) + receiver.astype(jnp.float32)[None]
     value, slope = activation(enc_pre)
     return (jnp.sum(value * live_mask[..., None], axis=0), slope * live_mask[..., None])
+
+
+STRIDES = (16, 4, 1)
+ORDERS = ((0, 1, 2), (1, 2, 0), (2, 0, 1))
+
+
+def remote(src, dst, sems, target):
+    return pltpu.make_async_remote_copy(
+        src_ref=src,
+        dst_ref=dst,
+        send_sem=sems.at[0],
+        recv_sem=sems.at[1],
+        device_id=target,
+        device_id_type=pl.DeviceIdType.MESH,
+    )
+
+
+def sum_kernel(
+    grads, gain, out, gain_out, pair_in, part, r1, s2, r2, s3, r3, gain_in, gain_held,
+    pair_sem, rs_sem, ag_sem, last_sem, gain_sem
+):
+    core = lax.axis_index("dp")
+    place = lax.axis_index("graph")
+    coords = [lax.rem(place // stride, 4) for stride in STRIDES]
+
+    def peer(axis, offset):
+        moved = lax.rem(coords[axis] + offset, 4)
+        return moved, {"graph": place + (moved - coords[axis]) * STRIDES[axis]}
+
+    barrier = pltpu.get_barrier_semaphore()
+    pl.semaphore_signal(
+        barrier, inc=1, device_id={"dp": 1 - core}, device_id_type=pl.DeviceIdType.MESH
+    )
+    for axis in range(3):
+        for offset in (1, 2, 3):
+            pl.semaphore_signal(
+                barrier,
+                inc=1,
+                device_id=peer(axis, offset)[1],
+                device_id_type=pl.DeviceIdType.MESH,
+            )
+    pl.semaphore_wait(barrier, 10)
+
+    pair = []
+    for p in range(3):
+        copy = remote(
+            grads.at[3 * (1 - core) + p], pair_in.at[p], pair_sem.at[p], {"dp": 1 - core}
+        )
+        copy.start()
+        pair.append(copy)
+    gain_copy = remote(gain, gain_in.at[9], gain_sem.at[9], {"dp": 1 - core})
+    gain_copy.start()
+    sent = [gain_copy]
+    stages = []
+    for p in range(3):
+        pair[p].wait_recv()
+        part[p] = (
+            grads[3 * core + p].astype(jnp.float32) + pair_in[p].astype(jnp.float32)
+        ).astype(jnp.bfloat16)
+        axis = ORDERS[p][0]
+        for offset in (1, 2, 3):
+            moved, target = peer(axis, offset)
+            copy = remote(
+                part.at[p, pl.ds(pl.multiple_of(moved * 128, 128), 128)],
+                r1.at[p, offset - 1],
+                rs_sem.at[p, offset - 1],
+                target,
+            )
+            copy.start()
+            stages.append(copy)
+    sent += pair
+    gain_copy.wait_recv()
+    gain_held[0] = gain[...] + gain_in[9]
+    for step in range(3):
+        copies = []
+        for offset in (1, 2, 3):
+            slot = 3 * step + offset - 1
+            copy = remote(
+                gain_held.at[step], gain_in.at[slot], gain_sem.at[slot], peer(step, offset)[1]
+            )
+            copy.start()
+            copies.append(copy)
+        if step == 0:
+            second = []
+            for p in range(3):
+                for copy in stages[3 * p : 3 * p + 3]:
+                    copy.wait_recv()
+                mine = coords[ORDERS[p][0]]
+                total = part[p, pl.ds(pl.multiple_of(mine * 128, 128), 128)].astype(jnp.float32)
+                for slot in range(3):
+                    total = total + r1[p, slot].astype(jnp.float32)
+                s2[p] = total.astype(jnp.bfloat16)
+                for offset in (1, 2, 3):
+                    moved, target = peer(ORDERS[p][1], offset)
+                    copy = remote(
+                        s2.at[p, pl.ds(pl.multiple_of(moved * 32, 32), 32)],
+                        r2.at[p, offset - 1],
+                        rs_sem.at[3 + p, offset - 1],
+                        target,
+                    )
+                    copy.start()
+                    second.append(copy)
+            sent += stages
+        if step == 1:
+            third = []
+            for p in range(3):
+                for copy in second[3 * p : 3 * p + 3]:
+                    copy.wait_recv()
+                mine = coords[ORDERS[p][1]]
+                total = s2[p, pl.ds(pl.multiple_of(mine * 32, 32), 32)].astype(jnp.float32)
+                for slot in range(3):
+                    total = total + r2[p, slot].astype(jnp.float32)
+                total = total.astype(jnp.bfloat16)
+                for quarter in range(4):
+                    s3[p, quarter] = total[
+                        16 * (quarter // 2) : 16 * (quarter // 2) + 16,
+                        256 * (quarter % 2) : 256 * (quarter % 2) + 256,
+                    ]
+                for offset in (1, 2, 3):
+                    moved, target = peer(ORDERS[p][2], offset)
+                    copy = remote(
+                        s3.at[p, moved], r3.at[p, offset - 1], rs_sem.at[6 + p, offset - 1], target
+                    )
+                    copy.start()
+                    third.append(copy)
+            sent += second
+        for copy in copies:
+            copy.wait_recv()
+        sent += copies
+        total = gain_held[step]
+        for slot in range(3):
+            total = total + gain_in[3 * step + slot]
+        if step < 2:
+            gain_held[step + 1] = total
+        else:
+            gain_out[...] = total
+    sent += third
+
+    def spread(p, level, slot, piece):
+        copies = []
+        for offset in (1, 2, 3):
+            copy = remote(
+                piece, piece, ag_sem.at[3 * level + p, offset - 1], peer(ORDERS[p][level], offset)[1]
+            )
+            copy.start()
+            copies.append(copy)
+        return copies
+
+    rows3, rows2, rows1 = [], [], []
+    wave = []
+    for p in range(3):
+        for copy in third[3 * p : 3 * p + 3]:
+            copy.wait_recv()
+        first, middle, last = [coords[axis] for axis in ORDERS[p]]
+        total = s3[p, last].astype(jnp.float32)
+        for slot in range(3):
+            total = total + r3[p, slot].astype(jnp.float32)
+        row1 = pl.multiple_of(first * 128, 128)
+        row2 = pl.multiple_of(first * 128 + middle * 32, 32)
+        row3 = pl.multiple_of(first * 128 + middle * 32 + (last // 2) * 16, 16)
+        column = pl.multiple_of(lax.rem(last, 2) * 256, 256)
+        whole = out.at[3 * core + p]
+        rows1.append(whole.at[pl.ds(row1, 128)])
+        rows2.append(whole.at[pl.ds(row2, 32)])
+        piece = whole.at[pl.ds(row3, 16), pl.ds(column, 256)]
+        piece[...] = total.astype(jnp.bfloat16)
+        wave.append(spread(p, 2, 0, piece))
+    for level, pieces in ((1, rows2), (0, rows1)):
+        following = []
+        for p in range(3):
+            for copy in wave[p]:
+                copy.wait_recv()
+            following.append(spread(p, level, 0, pieces[p]))
+            sent += wave[p]
+        wave = following
+    last = []
+    for p in range(3):
+        for copy in wave[p]:
+            copy.wait_recv()
+        copy = remote(
+            out.at[3 * core + p], out.at[3 * core + p], last_sem.at[p], {"dp": 1 - core}
+        )
+        copy.start()
+        last.append(copy)
+        sent += wave[p]
+    for copy in last:
+        copy.wait_recv()
+    sent += last
+    for copy in sent:
+        copy.wait_send()
+
+
+def sum_everywhere(grads, gain):
+    half = jnp.bfloat16
+    return pl.pallas_call(
+        sum_kernel,
+        out_shape=(
+            jax.ShapeDtypeStruct((6, 512, 512), half),
+            jax.ShapeDtypeStruct((8, 128), jnp.float32),
+        ),
+        in_specs=[pl.BlockSpec(memory_space=pltpu.VMEM)] * 2,
+        out_specs=[pl.BlockSpec(memory_space=pltpu.VMEM)] * 2,
+        scratch_shapes=[
+            pltpu.VMEM((3, 512, 512), half),
+            pltpu.VMEM((3, 512, 512), half),
+            pltpu.VMEM((3, 3, 128, 512), half),
+            pltpu.VMEM((3, 128, 512), half),
+            pltpu.VMEM((3, 3, 32, 512), half),
+            pltpu.VMEM((3, 4, 16, 256), half),
+            pltpu.VMEM((3, 3, 16, 256), half),
+            pltpu.VMEM((10, 8, 128), jnp.float32),
+            pltpu.VMEM((3, 8, 128), jnp.float32),
+            pltpu.SemaphoreType.DMA((3, 2)),
+            pltpu.SemaphoreType.DMA((9, 3, 2)),
+            pltpu.SemaphoreType.DMA((9, 3, 2)),
+            pltpu.SemaphoreType.DMA((3, 2)),
+            pltpu.SemaphoreType.DMA((10, 2)),
+        ],
+        compiler_params=pltpu.CompilerParams(
+            collective_id=0, has_side_effects=True, vmem_limit_bytes=48 * 1024 * 1024
+        ),
+    )(grads, gain)
 
 
 def shards(
@@ -187,21 +411,22 @@
         + dot_cols(send_cot, send_weight)
     )
     grid_grad = grid_total.astype(jnp.bfloat16)[None]
-    summed = lax.psum(
-        (recv_term, send_term, update_term, gain_term, msend_term, grecv_term, out_term),
-        ("dp", "graph"),
-    )
+    terms = (recv_term, send_term, update_term, msend_term, grecv_term, out_term)
+    stacked = jnp.stack([term.astype(jnp.bfloat16) for term in terms])
+    gain_rows = jnp.concatenate([gain_term.reshape(4, 128), jnp.zeros((4, 128), jnp.float32)])
+    totals, gain_total = sum_everywhere(stacked, gain_rows)
+    totals = totals.astype(jnp.float32)
     factor = 1.0 / math.sqrt(grid_rows * lax.axis_size("graph") * lax.axis_size("dp"))
     return (
         grid_grad,
         mesh_grad,
-        summed[0] * factor,
-        summed[1] * factor,
-        summed[2] * factor,
-        summed[3] * factor,
-        summed[4] * factor,
-        summed[5] * factor,
-        summed[6] * factor,
+        totals[0] * factor,
+        totals[1] * factor,
+        totals[2] * factor,
+        gain_total[:4].reshape(512) * factor,
+        totals[3] * factor,
+        totals[4] * factor,
+        totals[5] * factor,
     )
 
 

time: 419 us -> 282 us (0.67)
  blocking collectives: 84.1 us -> 0 us
  waiting for transfers between devices: 87.4 us -> 4.75 us
  Pallas kernels: 0 us -> 63.1 us
  matrix products: 80.4 us -> 66.6 us
  between operations: 14.7 us -> 1.26 us
  local copies, waits for them, and re-layouts: 53.6 us -> 43 us
    psum x1 -> x0, blocking collectives: 84.1 us -> none  [shards(): lax.psum((recv_term, send_term, update_term, gain_term, msend_term, grecv...]
    psum x1 -> x0, waiting for transfers between devices: 81 us -> none  [shards(): lax.psum((recv_term, send_term, update_term, gain_term, msend_term, grecv...]
    pallas_call x0 -> x1, Pallas kernels: none -> 63.1 us  [sum_everywhere(): pl.pallas_call(sum_kernel, out_shape=(jax.ShapeDtypeStruct((6, 512, 512),...]
    dot_general x6, matrix products: 15.6 us -> 4.88 us  [dot_rows(): lax.dot_general(left, right, (((0,), (0,)), ((), ())), preferred_element_...]
    unnamed x76 -> x66, local copies, waits for them, and re-layouts: 15.9 us -> 6.58 us
    mul x4 -> x2, other arithmetic: 8.81 us -> 3.82 us  [the longest x1 3.24 us: shards(): totals[5] * factor]
  transfers between devices with their start and end apart: 9 -> 8, of which waited for: 3 -> 1; matrix products, arithmetic and copies ran while one was open for 12% -> 16% of each run, Pallas kernels for 0% -> 0%
where the time goes in v1:
time: 282 us; the launch traced here: 280 us
  other arithmetic  67.3 us (24%)
  matrix products  66.6 us (24%)
  Pallas kernels  63.1 us (22%)
  local copies, waits for them, and re-layouts  43 us (15%)
  starting transfers between devices  23.3 us (8%)
  loops' own time  10.9 us (4%)
  waiting for transfers between devices  4.75 us (2%)
    pallas_call x1, Pallas kernels, sum_everywhere(): pl.pallas_call(sum_kernel, out_shape=(jax.ShapeDtypeStruct((6, 512, 512),...  63.1 us
    dot_general x6, matrix products, one_block(): jnp.einsum('smw,smd->wd', selector, part_values, preferred_element_type=j...  19.3 us
    dot_general x6, matrix products, one_block(): jnp.einsum('smw,wd->smd', selector, window, preferred_element_type=jnp.fl...  17.8 us
    ppermute x4, starting transfers between devices, with_halo(): lax.ppermute(lax.slice_in_dim(block, block.shape[dim] - width, None, axis...  17.5 us
    dot_general x6, matrix products, dot_cols(): lax.dot_general(left, right, (((1,), (1,)), ((), ())), preferred_element_...  16.9 us
    convert_element_type x1, other arithmetic, shards(): (sum_cot[None] * dec_slope).astype(jnp.bfloat16)  11.2 us
    convert_element_type x1, local copies, waits for them, and re-layouts, shards(): dec_pre = dec_rows.astype(jnp.float32) + grid_proj[None]  10.8 us
    dynamic_slice x12, local copies, waits for them, and re-layouts, window_take(): taken = lax.map(one_block, jnp.arange(blocks, dtype=jnp.int32))  9.64 us
  transfers between devices with their start and end apart: 8, of which 1 were waited for; matrix products, arithmetic and copies ran while one was open for 16% of the time, Pallas kernels for 0%

profile of v1, /device:TPU:1, one launch (start us, length us, event | category | flops | bytes accessed | tf_op | source)
XLA Modules:
  0.0 280.1 jit_solution(10299776128403982711)
XLA Ops:
  0.7 1.6 copy-done
  2.2 2.3 convolution_convert_fusion.1
  4.5 1.3 copy-done.11
  6.7 4.7 %collective-permute-start = (bf16[256,512]{1,0:T(8,128)(2,1)}, bf16[256,512]{1,0:T(8,128)(2,1)}, u32[]{:S(2)}, u32[]{:S(2)}) collective-permute-start(bf16[256,512]{1,0:T(8,128)(2,1)} %get-tuple-element.383), channel_id=1, source_target_pairs={{0,1},{1,2},{2,3},{3,4},{4,5},{5,6},{6,7},{7,8},{8,9},{9,10},{10,1... | collective-permute-start | bytes 786440 | tf_op jit(solution)/shard_map/ppermute | solution.py:20
  11.4 1.3 collective-permute-start.1
  12.7 3.2 %fusion.49 = f32[2048,512]{1,0:T(8,128)} fusion(bf16[512,512]{1,0:T(8,128)(2,1)S(1)} %copy-done.13, bf16[1,2048,512]{2,1,0:T(8,128)(2,1)S(1)} %copy-done), kind=kOutput, calls=%fused_computation.65 | convolution fusion | flops 1073741824 | bytes 6815744 | tf_op jit(solution)/shard_map/dot_general | solution.py:375
  17.2 5.0 %fusion.54 = f32[2048,512]{1,0:T(8,128)} fusion(bf16[512,512]{1,0:T(8,128)(2,1)} %param.41, bf16[1,2048,512]{2,1,0:T(8,128)(2,1)} %param.31), kind=kOutput, calls=%fused_computation.70 | convolution fusion | flops 1073741824 | bytes 6815744 | tf_op jit(solution)/shard_map/dot_general | solution.py:40
  23.2 3.5 %pad_maximum_fusion = bf16[2560,512]{1,0:T(8,128)(2,1)} fusion(bf16[256,512]{1,0:T(8,128)(2,1)} %collective-permute-done.1, bf16[2048,512]{1,0:T(8,128)(2,1)} %copy-done.11, bf16[256,512]{1,0:T(8,128)(2,1)} %collective-permute-done), kind=kLoop, calls=%fused_computation.60 | loop fusion | flops 7864320 | bytes 5242880 | tf_op jit(solution)/shard_map/concatenate | solution.py:24
  26.7 14.3 %while.52 = (s32[]{:T(128)}, bf16[2,12,128,512]{3,2,1,0:T(8,128)(2,1)}, s32[2]{0:T(128)S(1)}, s32[12,256]{1,0:T(8,128)S(1)}, bf16[2560,512]{1,0:T(8,128)(2,1)}, ...) while((s32[]{:T(128)}, bf16[2,12,128,512]{3,2,1,0:T(8,128)(2,1)}, ...), condition=%wide.region_1.2_spmd, body=%wide.region_0.1_spmd.sunk | while | flops 2419066368 | bytes 3164897 | solution.py:63
  28.6 5.2 %bitcast_dynamic-update-slice_fusion.4 = bf16[2,12,128,512]{3,2,1,0:T(8,128)(2,1)} fusion(bf16[2,12,128,512]{3,2,1,0:T(8,128)(2,1)} %get-tuple-element.528, s32[]{:T(128)} %get-tuple-element.527, bf16[2560,512]{1,0:T(8,128)(2,1)} %get-tuple-element.542, s32[]{:T(128)S(6)} %select_n.84, s32[12,128]{1,0:T(8,128)S(1)} %dynamic-slice_subtract_fusion.8), kind=kOutput, calls=%fused_computation.4.clone.1 | convolution fusion | flops 2419064832 | bytes 3152388 | tf_op jit(solution)/shard_map/while/body/eval_jaxpr/smw,wd->smd/dot_general | solution.py:59
  35.7 5.2 %bitcast_dynamic-update-slice_fusion.4 = bf16[2,12,128,512]{3,2,1,0:T(8,128)(2,1)} fusion(bf16[2,12,128,512]{3,2,1,0:T(8,128)(2,1)} %get-tuple-element.528, s32[]{:T(128)} %get-tuple-element.527, bf16[2560,512]{1,0:T(8,128)(2,1)} %get-tuple-element.542, s32[]{:T(128)S(6)} %select_n.84, s32[12,128]{1,0:T(8,128)S(1)} %dynamic-slice_subtract_fusion.8), kind=kOutput, calls=%fused_computation.4.clone.1 | convolution fusion | flops 2419064832 | bytes 3152388 | tf_op jit(solution)/shard_map/while/body/eval_jaxpr/smw,wd->smd/dot_general | solution.py:59
  41.0 3.6 %fusion.43 = bf16[2,128,512]{2,1,0:T(8,128)(2,1)S(1)} fusion(bf16[2,12,128,512]{3,2,1,0:T(8,128)(2,1)} %get-tuple-element.327, f32[12,2,128]{2,0,1:T(8,128)S(1)} %fusion.107, f32[2,128,512]{2,1,0:T(8,128)S(1)} %bitcast.215), kind=kLoop, calls=%fused_computation.56 | loop fusion | flops 12451840 | bytes 3944448 | tf_op jit(solution)/shard_map/reduce_sum | solution.py:98
  44.5 1.5 multiply_reduce_fusion.2
  46.6 4.0 %collective-permute-start.2 = (bf16[64,512]{1,0:T(8,128)(2,1)S(1)}, bf16[64,512]{1,0:T(8,128)(2,1)S(1)}, u32[]{:S(2)}, u32[]{:S(2)}) collective-permute-start(bf16[64,512]{1,0:T(8,128)(2,1)S(1)} %get-tuple-element.387), channel_id=1, source_target_pairs={{0,1},{1,2},{2,3},{3,4},{4,5},{5,6},{6,7},{7,8},{8,9},{9,10},{10,1... | collective-permute-start | bytes 196616 | tf_op jit(solution)/shard_map/ppermute | solution.py:20
  50.6 1.5 collective-permute-start.3
  52.1 0.8 convert_bitcast_fusion.1
  53.0 3.4 %copy.23 = f32[12,2,128,512]{3,2,1,0:T(8,128)} copy(f32[12,2,128,512]{3,2,0,1:T(8,128)S(1)} %convert_bitcast_fusion.1) | data formatting | bytes 12582912 | tf_op jit(solution)/shard_map/convert_element_type | solution.py:96
  56.4 15.2 %while.53 = (s32[]{:T(128)}, bf16[4,3,512,512]{3,2,1,0:T(8,128)(2,1)}, s32[4]{0:T(128)S(1)}, s32[3,2048]{1,0:T(4,128)}, bf16[384,512]{1,0:T(8,128)(2,1)S(1)}, /*...) while((s32[]{:T(128)}, ...), condition=%wide.region_5.6_spmd, body=%wide.region_4.5_spmd.sunk | while | flops 303072800 | bytes 1790834 | solution.py:63
  58.4 1.8 bitcast_dynamic-update-slice_fusion.5
  62.2 1.8 bitcast_dynamic-update-slice_fusion.5
  66.0 1.8 bitcast_dynamic-update-slice_fusion.5
  69.8 1.9 bitcast_dynamic-update-slice_fusion.5
  71.6 9.0 %convert_bitcast_fusion = f32[3,4,512,512]{3,2,0,1:T(8,128)} fusion(bf16[4,3,512,512]{3,2,1,0:T(8,128)(2,1)} %get-tuple-element.328), kind=kLoop, calls=%fused_computation.35 | loop fusion | flops 3145728 | bytes 18874368 | tf_op jit(solution)/shard_map/convert_element_type | solution.py:377
  80.7 10.8 %copy.22 = f32[3,4,512,512]{3,2,1,0:T(8,128)} copy(f32[3,4,512,512]{3,2,0,1:T(8,128)} %convert_bitcast_fusion) | data formatting | bytes 25165824 | tf_op jit(solution)/shard_map/convert_element_type | solution.py:377
  91.5 11.2 %multiply_convert_fusion = bf16[3,2048,512]{2,1,0:T(8,128)(2,1)} fusion(f32[3,4,512,512]{3,2,1,0:T(8,128)} %copy.22, f32[2048,512]{1,0:T(8,128)S(1)} %copy-done.1, f32[2048,512]{1,0:T(8,128)} %fusion.54), kind=kLoop, calls=%fused_computation.43 | loop fusion | flops 31457280 | bytes 27262976 | tf_op jit(solution)/shard_map/convert_element_type | solution.py:382
  103.2 20.0 %while.54 = (s32[]{:T(128)}, f32[384,512]{1,0:T(8,128)S(1)}, s32[4]{0:T(128)}, s32[3,2048]{1,0:T(4,128)}, bf16[3,2048,512]{2,1,0:T(8,128)(2,1)}, /*index=5*/s32[...) while((s32[]{:T(128)}, f32[384,512]{1,0:T(8,128)S(1)}, ...), condition=%wide.region_8.9_spmd, body=%wide.region_7.8_spmd.sunk | while | flops 302384672 | bytes 3164538 | solution.py:79
  103.3 1.2 dynamic_slice.133
  105.9 1.9 fusion.146
  108.2 1.2 dynamic_slice.133
  110.9 1.9 fusion.146
  113.2 1.2 dynamic_slice.133
  115.8 1.9 fusion.146
  118.2 1.2 dynamic_slice.133
  120.8 1.9 fusion.146
  123.9 4.0 %collective-permute-start.4 = (f32[64,512]{1,0:T(8,128)}, f32[64,512]{1,0:T(8,128)S(1)}, u32[]{:S(2)}, u32[]{:S(2)}) collective-permute-start(f32[64,512]{1,0:T(8,128)} %get-tuple-element.386), channel_id=1, source_target_pairs={{0,1},{1,2},{2,3},{3,4},{4,5},{5,6},{6,7},{7,8},{8,9},{9,10},{10,1... | collective-permute-start | bytes 393224 | tf_op jit(solution)/shard_map/ppermute | solution.py:20
  127.9 1.5 collective-permute-start.5
  129.4 8.2 %fusion.35 = bf16[4,512,512]{2,1,0:T(8,128)(2,1)} fusion(bf16[4,3,512,512]{3,2,1,0:T(8,128)(2,1)} %get-tuple-element.328, f32[4,512,512]{2,1,0:T(8,128)} %bitcast.213), kind=kLoop, calls=%fused_computation.44 | loop fusion | flops 20971520 | bytes 12582912 | tf_op jit(solution)/shard_map/reduce_sum | solution.py:379
  137.6 0.8 slice.133
  138.4 5.8 %reduce_sum.71 = bf16[2048,512]{1,0:T(8,128)(2,1)} reduce(bf16[3,2048,512]{2,1,0:T(8,128)(2,1)} %get-tuple-element.660, bf16[]{:T(256)} %constant.345.clone.1), dimensions={0}, to_apply=%region_6.7 | reduce | flops 2097152 | bytes 8388610 | tf_op jit(solution)/shard_map/reduce_sum | solution.py:383
  144.9 1.6 fusion.103
  146.4 1.8 multiply_reduce_fusion
  148.3 1.2 multiply_convert_fusion.2
  150.5 5.6 %multiply_convert_fusion.1 = bf16[12,256,512]{2,1,0:T(8,128)(2,1)} fusion(f32[12,2,128,512]{3,2,1,0:T(8,128)} %copy.23, f32[12,256]{1,0:T(8,128)S(1)} %copy-done.26, f32[256,512]{1,0:T(8,128)S(1)} %copy-done.10, f32[256,512]{1,0:T(8,128)S(1)} %fusion.114), kind=kLoop, calls=%fused_computation.55 | loop fusion | flops 17301504 | bytes 10498048 | tf_op jit(solution)/shard_map/convert_element_type | solution.py:398
  156.1 3.0 %broadcast_in_dim.34 = f32[2560,512]{1,0:T(8,128)} broadcast(f32[]{:T(128)} %constant.351.clone.1), dimensions={} | broadcast | bytes 5242884 | tf_op jit(solution)/shard_map/broadcast_in_dim | solution.py:78
  159.1 15.6 %while.55 = (s32[]{:T(128)}, f32[2560,512]{1,0:T(8,128)}, s32[2]{0:T(128)S(1)}, s32[12,256]{1,0:T(8,128)S(1)}, bf16[12,256,512]{2,1,0:T(8,128)(2,1)}, /*index=5*...) while((s32[]{:T(128)}, f32[2560,512]{1,0:T(8,128)}, ...), condition=%wide.region_11.12_spmd, body=%wide.region_10.11_spmd.sunk | while | flops 2419066368 | bytes 7882981 | solution.py:79
  161.0 5.9 %fusion.148 = f32[2560,512]{1,0:T(8,128)} fusion(f32[2560,512]{1,0:T(8,128)} %get-tuple-element.639, s32[]{:T(128)S(6)} %select_n.92, s32[12,128]{1,0:T(8,128)S(1)} %dynamic-slice_subtract_fusion.11, bf16[12,256,512]{2,1,0:T(8,128)(2,1)} %get-tuple-element.653, s32[]{:T(128)S(6)} %select_n.93), kind=kOutput, calls=%fused_computation.30.clone.1 | convolution fusion | flops 2419064832 | bytes 7870472 | tf_op jit(solution)/shard_map/while/body/eval_jaxpr/smw,smd->wd/dot_general | solution.py:74
  168.8 5.9 %fusion.148 = f32[2560,512]{1,0:T(8,128)} fusion(f32[2560,512]{1,0:T(8,128)} %get-tuple-element.639, s32[]{:T(128)S(6)} %select_n.92, s32[12,128]{1,0:T(8,128)S(1)} %dynamic-slice_subtract_fusion.11, bf16[12,256,512]{2,1,0:T(8,128)(2,1)} %get-tuple-element.653, s32[]{:T(128)S(6)} %select_n.93), kind=kOutput, calls=%fused_computation.30.clone.1 | convolution fusion | flops 2419064832 | bytes 7870472 | tf_op jit(solution)/shard_map/while/body/eval_jaxpr/smw,smd->wd/dot_general | solution.py:74
  174.7 2.2 fusion.109
  176.9 4.8 %collective-permute-start.6 = (f32[256,512]{1,0:T(8,128)}, f32[256,512]{1,0:T(8,128)}, u32[]{:S(2)}, u32[]{:S(2)}) collective-permute-start(f32[256,512]{1,0:T(8,128)} %get-tuple-element.382), channel_id=1, source_target_pairs={{0,1},{1,2},{2,3},{3,4},{4,5},{5,6},{6,7},{7,8},{8,9},{9,10},{10,1... | collective-permute-start | bytes 1572872 | tf_op jit(solution)/shard_map/ppermute | solution.py:20
  181.7 4.9 %fusion.113 = f32[2048,512]{1,0:T(8,128)} fusion(bf16[2048,512]{1,0:T(8,128)(2,1)} %reduce_sum.71, bf16[512,512]{1,0:T(8,128)(2,1)S(1)} %copy-done.14), kind=kOutput, calls=%fused_computation.140 | convolution fusion | flops 1073741824 | bytes 6815744 | tf_op jit(solution)/shard_map/dot_general | solution.py:40
  186.6 2.4 reduce_sum.73
  189.0 1.6 collective-permute-start.7
  190.6 2.1 fusion.91
  192.7 2.7 slice.138
  195.7 1.3 add_dynamic-update-slice_fusion
  197.0 4.7 %collective-permute-done.7 = f32[256,512]{1,0:T(8,128)S(1)} collective-permute-done((f32[256,512]{1,0:T(8,128)}, f32[256,512]{1,0:T(8,128)S(1)}, u32[]{:S(2)}, u32[]{:S(2)}) %collective-permute-start.7) | collective-permute-done | bytes 524320 | tf_op jit(solution)/shard_map/ppermute | solution.py:23
  202.0 1.3 fusion.80
  204.0 1.3 fusion.74
  205.9 1.3 fusion.86.grads
  207.2 1.6 copy-done.12
  208.8 63.1 %shard_map.196 = (bf16[6,512,512]{2,1,0:T(8,128)(2,1)S(1)}, f32[8,128]{1,0:T(8,128)S(1)}) custom-call(bf16[6,512,512]{2,1,0:T(8,128)(2,1)} %copy-done.12, f32[8,128]{1,0:T(8,128)S(1)} %concatenate.19.gain), custom_call_target="tpu_custom_call" | custom-call | tf_op jit(solution)/shard_map/pallas_call | solution.py:293
  271.9 0.9 convert_element_type.188
  272.8 3.2 %fusion.92 = (f32[512,512]{1,0:T(8,128)}, f32[512,512]{1,0:T(8,128)}, f32[512,512]{1,0:T(8,128)}, f32[512,512]{1,0:T(8,128)}, f32[512,512]{1,0:T(8,128)}, /*index=5*/f32[512,512]{1,0:T(8,128)}) fusion(f32[6,512,512]{2,1,0:T(8,128)S(1)} %convert_element_type.188), kind=kLoop, calls=%fused_computation.97 | loop fusion | flops 1572864 | bytes 12582912 | tf_op jit(solution)/shard_map/mul | solution.py:429
  277.3 2.9 %fusion.44 = bf16[1,2048,512]{2,1,0:T(8,128)(2,1)} fusion(bf16[512,512]{1,0:T(8,128)(2,1)S(1)} %copy-done.25, f32[2048,512]{1,0:T(8,128)S(1)} %copy-done.2, bf16[1,2048,512]{2,1,0:T(8,128)(2,1)S(1)} %copy-done.3, f32[2048,512]{1,0:T(8,128)S(1)} %fusion.100), kind=kOutput, calls=%fused_computation.59 | convolution fusion | flops 1078984704 | bytes 13107200 | tf_op jit(solution)/shard_map/dot_general | solution.py:40
  (123 shorter events, 21.6 us)
Async XLA Ops:
  0.6 1.6 copy-start
  0.7 12.0 %copy-start.13 = (bf16[512,512]{1,0:T(8,128)(2,1)S(1)}, bf16[512,512]{1,0:T(8,128)(2,1)}, u32[]{:S(2)}) copy-start(bf16[512,512]{1,0:T(8,128)(2,1)} %param.40) | copy-start | bytes 1572868
  4.5 1.3 copy-start.11
  6.7 16.5 %collective-permute-start = (bf16[256,512]{1,0:T(8,128)(2,1)}, bf16[256,512]{1,0:T(8,128)(2,1)}, u32[]{:S(2)}, u32[]{:S(2)}) collective-permute-start(bf16[256,512]{1,0:T(8,128)(2,1)} %get-tuple-element.383), channel_id=1, source_target_pairs={{0,1},{1,2},{2,3},{3,4},{4,5},{5,6},{6,7},{7,8},{8,9},{9,10},{10,1... | collective-permute-start | bytes 786440 | tf_op jit(solution)/shard_map/ppermute | solution.py:20
  11.4 11.8 %collective-permute-start.1 = (bf16[256,512]{1,0:T(8,128)(2,1)}, bf16[256,512]{1,0:T(8,128)(2,1)}, u32[]{:S(2)}, u32[]{:S(2)}) collective-permute-start(bf16[256,512]{1,0:T(8,128)(2,1)} %get-tuple-element.384), channel_id=1, source_target_pairs={{1,0},{2,1},{3,2},{4,3},{5,4},{6,5},{7,6},{8,7},{9,8},{10,9},{11,1... | collective-permute-start | bytes 786440 | tf_op jit(solution)/shard_map/ppermute | solution.py:23
  12.7 3.3 %copy-start.31 = (s32[256]{0:T(256)S(1)}, s32[256]{0:T(256)}, u32[]{:S(2)}) copy-start(s32[256]{0:T(256)} %param.33) | copy-start | bytes 3076
  12.7 3.9 %copy-start.30 = (s32[12,256]{1,0:T(8,128)S(1)}, s32[12,256]{1,0:T(8,128)}, u32[]{:S(2)}) copy-start(s32[12,256]{1,0:T(8,128)} %param.32) | copy-start | bytes 36868
  12.7 3.9 %copy-start.28 = (s32[3,2048]{1,0:T(4,128)S(1)}, s32[3,2048]{1,0:T(4,128)}, u32[]{:S(2)}) copy-start(s32[3,2048]{1,0:T(4,128)} %param.34) | copy-start | bytes 73732
  17.2 5.0 %copy-start.32 = (bf16[512]{0:T(512)(128)(2,1)S(1)}, bf16[512]{0:T(512)(128)(2,1)}, u32[]{:S(2)}) copy-start(bf16[512]{0:T(512)(128)(2,1)} %param.38) | copy-start | bytes 3076
  17.2 5.6 %copy-start.16 = (bf16[512,512]{1,0:T(8,128)(2,1)S(1)}, bf16[512,512]{1,0:T(8,128)(2,1)}, u32[]{:S(2)}) copy-start(bf16[512,512]{1,0:T(8,128)(2,1)} %param.35) | copy-start | bytes 1572868
  17.2 5.6 %copy-start.18 = (bf16[1,256,512]{2,1,0:T(8,128)(2,1)S(1)}, bf16[1,256,512]{2,1,0:T(8,128)(2,1)}, u32[]{:S(2)}) copy-start(bf16[1,256,512]{2,1,0:T(8,128)(2,1)} %param.30) | copy-start | bytes 786436
  23.1 17.8 %copy-start.9 = (f32[256,512]{1,0:T(8,128)}, f32[256,512]{1,0:T(8,128)S(1)}, u32[]{:S(2)}) copy-start(f32[256,512]{1,0:T(8,128)S(1)} %fusion.90) | copy-start | bytes 1572868
  41.0 5.1 %copy-start.19 = (bf16[1,256,512]{2,1,0:T(8,128)(2,1)S(1)}, bf16[1,256,512]{2,1,0:T(8,128)(2,1)}, u32[]{:S(2)}) copy-start(bf16[1,256,512]{2,1,0:T(8,128)(2,1)} %param.30) | copy-start | bytes 786436
  41.0 5.2 %copy-start.27 = (f32[512]{0:T(512)S(1)}, f32[512]{0:T(512)}, u32[]{:S(2)}) copy-start(f32[512]{0:T(512)} %convert_element_type.152) | copy-start | bytes 6148
  41.0 5.3 %copy-start.15 = (bf16[512,512]{1,0:T(8,128)(2,1)S(1)}, bf16[512,512]{1,0:T(8,128)(2,1)}, u32[]{:S(2)}) copy-start(bf16[512,512]{1,0:T(8,128)(2,1)} %param.39) | copy-start | bytes 1572868
  41.0 11.1 %copy-start.5 = (bf16[2,12,128,512]{3,2,1,0:T(8,128)(2,1)S(1)}, bf16[2,12,128,512]{3,2,1,0:T(8,128)(2,1)}, u32[]{:S(2)}) copy-start(bf16[2,12,128,512]{3,2,1,0:T(8,128)(2,1)} %get-tuple-element.327) | copy-start | bytes 9437188
  44.5 6.1 %copy-start.23 = (bf16[2,128,512]{2,1,0:T(8,128)(2,1)}, bf16[2,128,512]{2,1,0:T(8,128)(2,1)S(1)}, u32[]{:S(2)}) copy-start(bf16[2,128,512]{2,1,0:T(8,128)(2,1)S(1)} %fusion.43) | copy-start | bytes 786436
  46.1 4.6 %copy-start.6 = (f32[256,512]{1,0:T(8,128)}, f32[256,512]{1,0:T(8,128)S(1)}, u32[]{:S(2)}) copy-start(f32[256,512]{1,0:T(8,128)S(1)} %get-tuple-element.390) | copy-start | bytes 1572868
  46.1 6.9 %copy-start.29 = (f32[256]{0:T(256)}, f32[256]{0:T(256)S(1)}, u32[]{:S(2)}) copy-start(f32[256]{0:T(256)S(1)} %add_rsqrt_fusion) | copy-start | bytes 3076
  46.6 9.8 %collective-permute-start.2 = (bf16[64,512]{1,0:T(8,128)(2,1)S(1)}, bf16[64,512]{1,0:T(8,128)(2,1)S(1)}, u32[]{:S(2)}, u32[]{:S(2)}) collective-permute-start(bf16[64,512]{1,0:T(8,128)(2,1)S(1)} %get-tuple-element.387), channel_id=1, source_target_pairs={{0,1},{1,2},{2,3},{3,4},{4,5},{5,6},{6,7},{7,8},{8,9},{9,10},{10,1... | collective-permute-start | bytes 196616 | tf_op jit(solution)/shard_map/ppermute | solution.py:20
  50.6 5.7 %collective-permute-start.3 = (bf16[64,512]{1,0:T(8,128)(2,1)S(1)}, bf16[64,512]{1,0:T(8,128)(2,1)S(1)}, u32[]{:S(2)}, u32[]{:S(2)}) collective-permute-start(bf16[64,512]{1,0:T(8,128)(2,1)S(1)} %get-tuple-element.388), channel_id=1, source_target_pairs={{1,0},{2,1},{3,2},{4,3},{5,4},{6,5},{7,6},{8,7},{9,8},{10,9},{11,1... | collective-permute-start | bytes 196616 | tf_op jit(solution)/shard_map/ppermute | solution.py:23
  80.7 10.8 %copy-start.1 = (f32[2048,512]{1,0:T(8,128)S(1)}, f32[2048,512]{1,0:T(8,128)}, u32[]{:S(2)}) copy-start(f32[2048,512]{1,0:T(8,128)} %fusion.49) | copy-start | bytes 12582916
  123.9 20.3 %collective-permute-start.4 = (f32[64,512]{1,0:T(8,128)}, f32[64,512]{1,0:T(8,128)S(1)}, u32[]{:S(2)}, u32[]{:S(2)}) collective-permute-start(f32[64,512]{1,0:T(8,128)} %get-tuple-element.386), channel_id=1, source_target_pairs={{0,1},{1,2},{2,3},{3,4},{4,5},{5,6},{6,7},{7,8},{8,9},{9,10},{10,1... | collective-permute-start | bytes 393224 | tf_op jit(solution)/shard_map/ppermute | solution.py:20
  127.9 17.0 %collective-permute-start.5 = (f32[64,512]{1,0:T(8,128)S(1)}, f32[64,512]{1,0:T(8,128)S(1)}, u32[]{:S(2)}, u32[]{:S(2)}) collective-permute-start(f32[64,512]{1,0:T(8,128)S(1)} %get-tuple-element.385), channel_id=1, source_target_pairs={{1,0},{2,1},{3,2},{4,3},{5,4},{6,5},{7,6},{8,7},{9,8},{10,9},{11,1... | collective-permute-start | bytes 393224 | tf_op jit(solution)/shard_map/ppermute | solution.py:23
  144.2 6.0 %copy-start.17 = (bf16[512,512]{1,0:T(8,128)(2,1)S(1)}, bf16[512,512]{1,0:T(8,128)(2,1)}, u32[]{:S(2)}) copy-start(bf16[512,512]{1,0:T(8,128)(2,1)} %param.37) | copy-start | bytes 1572868
  144.2 6.4 %copy-start.10 = (f32[256,512]{1,0:T(8,128)S(1)}, f32[256,512]{1,0:T(8,128)}, u32[]{:S(2)}) copy-start(f32[256,512]{1,0:T(8,128)} %copy-done.9) | copy-start | bytes 1572868
  144.2 6.4 %copy-start.26 = (f32[12,256]{1,0:T(8,128)S(1)}, f32[12,256]{1,0:T(8,128)}, u32[]{:S(2)}) copy-start(f32[12,256]{1,0:T(8,128)} %fusion.108) | copy-start | bytes 36868
  149.5 0.7 copy-start.21
  159.1 22.6 %copy-start.14 = (bf16[512,512]{1,0:T(8,128)(2,1)S(1)}, bf16[512,512]{1,0:T(8,128)(2,1)}, u32[]{:S(2)}) copy-start(bf16[512,512]{1,0:T(8,128)(2,1)} %param.40) | copy-start | bytes 1572868
  176.9 18.8 %collective-permute-start.6 = (f32[256,512]{1,0:T(8,128)}, f32[256,512]{1,0:T(8,128)}, u32[]{:S(2)}, u32[]{:S(2)}) collective-permute-start(f32[256,512]{1,0:T(8,128)} %get-tuple-element.382), channel_id=1, source_target_pairs={{0,1},{1,2},{2,3},{3,4},{4,5},{5,6},{6,7},{7,8},{8,9},{9,10},{10,1... | collective-permute-start | bytes 1572872 | tf_op jit(solution)/shard_map/ppermute | solution.py:20
  189.0 12.7 %collective-permute-start.7 = (f32[256,512]{1,0:T(8,128)}, f32[256,512]{1,0:T(8,128)S(1)}, u32[]{:S(2)}, u32[]{:S(2)}) collective-permute-start(f32[256,512]{1,0:T(8,128)} %get-tuple-element.381), channel_id=1, source_target_pairs={{1,0},{2,1},{3,2},{4,3},{5,4},{6,5},{7,6},{8,7},{9,8},{10,9},{11,1... | collective-permute-start | bytes 1572872 | tf_op jit(solution)/shard_map/ppermute | solution.py:23
  192.7 2.7 copy-start.20
  197.0 6.2 %copy-start.22 = (bf16[256,512]{1,0:T(8,128)(2,1)S(1)}, bf16[256,512]{1,0:T(8,128)(2,1)}, u32[]{:S(2)}) copy-start(bf16[256,512]{1,0:T(8,128)(2,1)} %copy-done.21) | copy-start | bytes 786436
  197.0 6.2 %copy-start.24 = (bf16[2,128,512]{2,1,0:T(8,128)(2,1)S(1)}, bf16[2,128,512]{2,1,0:T(8,128)(2,1)}, u32[]{:S(2)}) copy-start(bf16[2,128,512]{2,1,0:T(8,128)(2,1)} %copy-done.23) | copy-start | bytes 786436
  201.9 1.7 copy-start.8
  201.9 2.0 copy-start.4
  203.6 1.7 copy-start.3
  203.6 2.2 copy-start.7
  207.1 1.6 copy-start.12
  272.8 4.4 %copy-start.2 = (f32[2048,512]{1,0:T(8,128)S(1)}, f32[2048,512]{1,0:T(8,128)}, u32[]{:S(2)}) copy-start(f32[2048,512]{1,0:T(8,128)} %fusion.113) | copy-start | bytes 12582916
  272.8 4.5 %copy-start.25 = (bf16[512,512]{1,0:T(8,128)(2,1)S(1)}, bf16[512,512]{1,0:T(8,128)(2,1)}, u32[]{:S(2)}) copy-start(bf16[512,512]{1,0:T(8,128)(2,1)} %param.36) | copy-start | bytes 1572868

commit v2 on v1

--- a/solution.py
+++ b/solution.py
@@ -10,92 +10,6 @@
 KE = 12
 GRIM = 256
 MRIM = 64
-
-
-def with_halo(block, sides, width):
-    for axis, dim in sides:
-        count = lax.axis_size(axis)
-        forward = [(i, i + 1) for i in range(count - 1)]
-        backward = [(target, source) for source, target in forward]
-        low = lax.ppermute(
-            lax.slice_in_dim(block, block.shape[dim] - width, None, axis=dim), axis, forward
-        )
-        high = lax.ppermute(lax.slice_in_dim(block, 0, width, axis=dim), axis, backward)
-        block = jnp.concatenate([low, block, high], axis=dim)
-    return block
-
-
-def activation(pre_value):
-    gate_sig = jax.nn.sigmoid(pre_value)
-    return (pre_value * gate_sig, gate_sig * (1.0 + pre_value * (1.0 - gate_sig)))
-
-
-def dot_rows(left, right):
-    return lax.dot_general(
-        left, right, (((0,), (0,)), ((), ())), preferred_element_type=jnp.float32
-    )
-
-
-def dot_cols(left, right):
-    return lax.dot_general(
-        left, right, (((1,), (1,)), ((), ())), preferred_element_type=jnp.float32
-    )
-
-
-def selector_block(index, number, block, numer, denom, width):
-    window_start = number * block * numer // denom
-    picked = lax.dynamic_slice_in_dim(index, number * block, block, 1) - window_start
-    selector = (picked[..., None] == jnp.arange(width, dtype=jnp.int32)).astype(jnp.bfloat16)
-    return (window_start, selector)
-
-
-def window_take(extended, index, block, numer, denom, width):
-    slots, columns = index.shape
-    blocks = columns // block
-
-    def one_block(number):
-        window_start, selector = selector_block(index, number, block, numer, denom, width)
-        window = lax.dynamic_slice_in_dim(extended, window_start, width, 0)
-        return jnp.einsum(
-            "smw,wd->smd", selector, window, preferred_element_type=jnp.float32
-        ).astype(jnp.bfloat16)
-
-    taken = lax.map(one_block, jnp.arange(blocks, dtype=jnp.int32))
-    return jnp.transpose(taken, (1, 0, 2, 3)).reshape(slots, columns, extended.shape[1])
-
-
-def window_add(total_rows, index, values, block, numer, denom, width):
-    columns = index.shape[1]
-    blocks = columns // block
-
-    def one_block(totals, number):
-        window_start, selector = selector_block(index, number, block, numer, denom, width)
-        part_values = lax.dynamic_slice_in_dim(values, number * block, block, 1)
-        added = jnp.einsum("smw,smd->wd", selector, part_values, preferred_element_type=jnp.float32)
-        current = lax.dynamic_slice_in_dim(totals, window_start, width, 0)
-        return (lax.dynamic_update_slice_in_dim(totals, current + added, window_start, 0), 0)
-
-    start_totals = jnp.zeros((total_rows, values.shape[2]), jnp.float32)
-    totals, unused = lax.scan(one_block, start_totals, jnp.arange(blocks, dtype=jnp.int32))
-    return totals
-
-
-def neighbour_rows(values, depth):
-    return with_halo(values, (("graph", 0),), depth)
-
-
-def return_rims(extended, depth):
-    rims = jnp.concatenate([extended[:depth], extended[-depth:]], 0)
-    arrived = with_halo(rims, (("graph", 0),), depth)
-    owned = extended[depth:-depth]
-    owned = owned.at[:depth].add(arrived[:depth])
-    return owned.at[-depth:].add(arrived[-depth:])
-
-
-def slot_forward(gathered, receiver, live_mask):
-    enc_pre = gathered.astype(jnp.float32) + receiver.astype(jnp.float32)[None]
-    value, slope = activation(enc_pre)
-    return (jnp.sum(value * live_mask[..., None], axis=0), slope * live_mask[..., None])
 
 
 STRIDES = (16, 4, 1)
@@ -320,6 +234,331 @@
     )(grads, gain)
 
 
+HALF = jnp.bfloat16
+FULL = jnp.float32
+NODES = 32
+DEPTH = KE * NODES
+REACH = NODES * 8 + 2 * GRIM
+CELLS = 512
+SPAN = CELLS // 8 + 2 * MRIM
+
+
+def dot(left, right, dims=((1,), (0,))):
+    return lax.dot_general(left, right, (dims, ((), ())), preferred_element_type=FULL)
+
+
+def loop(count, body, start=0):
+    lax.fori_loop(start, count, lambda step, carry: (body(step), carry)[1], 0)
+
+
+def rows_at(index, size):
+    return pl.ds(pl.multiple_of(index * size, size), size)
+
+
+def half_silu(half_pre):
+    bend = jnp.tanh(half_pre)
+    lifted = 1.0 + bend
+    value = half_pre * lifted
+    return value, lifted + value * (1.0 - bend)
+
+
+def local_kernel(
+    grid, mesh, cot, enc_col, enc_row, counts, dec_col, dec_row,
+    w_recv, w_send, w_update, gain, w_msend, w_grecv, w_out,
+    grid_grad, mesh_grad, terms, gain_rows,
+    send_ext, gp, sc, rp, taken, slope, agg, normed, inv, mlat, mesh_ext,
+    dcot, dsum, rcot, mc_ext, mesh_rim, lat, mcot, ucot, acot, ecot, rsum,
+    scot, rim_out, rim_in, edge, acc, sems,
+):
+    place = lax.axis_index("graph")
+    left = {"graph": lax.rem(place + 63, 64)}
+    right = {"graph": lax.rem(place + 1, 64)}
+    barrier = pltpu.get_barrier_semaphore()
+    for target in (left, right):
+        pl.semaphore_signal(
+            barrier, inc=1, device_id=target, device_id_type=pl.DeviceIdType.MESH
+        )
+    pl.semaphore_wait(barrier, 2)
+    sent = []
+
+    def exchange(index, low, low_target, high, high_target):
+        pair = [
+            remote(low, low_target, sems.at[index], left),
+            remote(high, high_target, sems.at[index + 1], right),
+        ]
+        for copy in pair:
+            copy.start()
+        sent.extend(pair)
+        return pair
+
+    def project(start, size):
+        send_ext[pl.ds(start + GRIM, size)] = (
+            dot(grid[pl.ds(start, size)], w_send[...]) * 0.5
+        ).astype(HALF)
+
+    project(0, GRIM)
+    project(2048 - GRIM, GRIM)
+    grid_halo = exchange(
+        0,
+        send_ext.at[pl.ds(GRIM, GRIM)],
+        send_ext.at[pl.ds(2048 + GRIM, GRIM)],
+        send_ext.at[pl.ds(2048, GRIM)],
+        send_ext.at[pl.ds(0, GRIM)],
+    )
+    loop(3, lambda step: project(pl.multiple_of(GRIM + step * 512, 256), 512))
+    rp[...] = dot(mesh[...], w_recv[...]).astype(HALF).astype(FULL) * 0.5
+
+    def dense(step):
+        rows = rows_at(step, 512)
+        gp[rows] = dot(grid[rows], w_grecv[...]) * 0.5
+        sc[rows] = dot(cot[rows], w_out[...], ((1,), (1,))) * 0.5
+
+    loop(4, dense)
+
+    def encode(number):
+        columns = lax.broadcasted_iota(jnp.int32, (NODES, REACH), 1) + number * (NODES * 8)
+        nodes = rows_at(number, NODES)
+        picks = enc_col[nodes]
+        selector = jnp.concatenate(
+            [
+                jnp.where(picks[:, k : k + 1] == columns, 1.0, 0.0).astype(HALF)
+                for k in range(KE)
+            ]
+        )
+        taken[pl.ds(0, DEPTH)] = dot(
+            selector, send_ext[pl.ds(pl.multiple_of(number * (NODES * 8), 256), REACH)]
+        )
+        for part in range(NODES // 16):
+            rows = pl.ds(pl.multiple_of(number * NODES + part * 16, 16), 16)
+            number_live = counts[rows]
+            receiver = rp[rows]
+            total = jnp.zeros((16, 512), FULL)
+            for k in range(KE):
+                at = k * NODES + part * 16
+                value, bend = half_silu(taken[at : at + 16] + receiver)
+                mask = jnp.where(number_live > k, 1.0, 0.0)
+                total = total + value * mask
+                slope[number, at : at + 16] = (bend * mask).astype(HALF)
+            agg[rows] = total.astype(HALF)
+
+    loop(7, encode, 1)
+    for copy in grid_halo:
+        copy.wait_recv()
+    loop(2, lambda step: encode(step * 7))
+
+    acot[...] = dot(agg[...], w_update[...])
+
+    def normalise(step):
+        rows = rows_at(step, 16)
+        update = acot[rows]
+        scale = lax.rsqrt(jnp.mean(update * update, axis=-1, keepdims=True) + 1e-06)
+        inv[rows] = jnp.broadcast_to(scale, (16, 128))
+        flat = update * scale
+        normed[rows] = flat
+        mlat[rows] = (mesh[rows].astype(FULL) + gain[...].astype(FULL) * flat).astype(HALF)
+
+    loop(16, normalise)
+    mesh_ext[pl.ds(MRIM, 256)] = (dot(mlat[...], w_msend[...]) * 0.5).astype(HALF)
+    mesh_halo = exchange(
+        2,
+        mesh_ext.at[pl.ds(MRIM, MRIM)],
+        mesh_ext.at[pl.ds(256 + MRIM, MRIM)],
+        mesh_ext.at[pl.ds(256, MRIM)],
+        mesh_ext.at[pl.ds(0, MRIM)],
+    )
+    mc_ext[...] = jnp.zeros_like(mc_ext)
+
+    def decode(number):
+        base = pl.multiple_of(number * (CELLS // 8), 64)
+        cells = rows_at(number, CELLS)
+        window = mesh_ext[pl.ds(base, SPAN)]
+        columns = lax.broadcasted_iota(jnp.int32, (CELLS, SPAN), 1) + base
+        picks = dec_col[cells]
+        for j in range(3):
+            selector = jnp.where(picks[:, j : j + 1] == columns, 1.0, 0.0).astype(HALF)
+            taken[pl.ds(j * CELLS, CELLS)] = dot(selector, window)
+
+        def cell_rows(step):
+            inner = rows_at(step, 16)
+            rows = pl.ds(pl.multiple_of(number * CELLS + step * 16, 16), 16)
+            own = gp[rows]
+            cotangent = sc[rows]
+            total = jnp.zeros((16, 512), FULL)
+            back = jnp.zeros((16, 512), FULL)
+            for j in range(3):
+                value, bend = half_silu(
+                    taken[pl.ds(pl.multiple_of(j * CELLS + step * 16, 16), 16)] + own
+                )
+                total = total + value
+                part = cotangent * bend
+                back = back + part
+                dcot[j, inner] = part.astype(HALF)
+            dsum[rows] = total.astype(HALF)
+            rcot[rows] = back.astype(HALF)
+
+        lax.fori_loop(0, CELLS // 16, lambda i, c: (cell_rows(i), c)[1], 0, unroll=4)
+        lines = lax.broadcasted_iota(jnp.int32, (SPAN, CELLS), 0) + base
+        added = mc_ext[pl.ds(base, SPAN)]
+        for j in range(3):
+            selector = jnp.where(dec_row[j, number] == lines, 1.0, 0.0).astype(HALF)
+            added = added + dot(selector, dcot[j])
+        mc_ext[pl.ds(base, SPAN)] = added
+
+    loop(3, decode, 1)
+    for copy in mesh_halo:
+        copy.wait_recv()
+    loop(2, lambda step: decode(step * 3))
+    mesh_back = exchange(
+        4,
+        mc_ext.at[pl.ds(0, MRIM)],
+        mesh_rim.at[1],
+        mc_ext.at[pl.ds(256 + MRIM, MRIM)],
+        mesh_rim.at[0],
+    )
+
+    def contract(slot, lefts, rights, count, size):
+        acc[...] = jnp.zeros_like(acc)
+
+        def piece(step):
+            rows = rows_at(step, size)
+            acc[...] += dot(lefts[rows], rights[rows], ((0,), (0,)))
+
+        loop(count, piece)
+        terms[slot] = acc[...].astype(HALF)
+
+    contract(5, dsum, cot, 4, 512)
+    contract(4, grid, rcot, 4, 512)
+
+    def first_part(step):
+        rows = rows_at(step, 512)
+        gp[rows] = cot[rows].astype(FULL) + dot(rcot[rows], w_grecv[...], ((1,), (1,)))
+
+    loop(4, first_part)
+    for copy in mesh_back:
+        copy.wait_recv()
+    mcot[pl.ds(0, MRIM)] = (mc_ext[pl.ds(MRIM, MRIM)] + mesh_rim[0]).astype(HALF)
+    mcot[pl.ds(MRIM, 128)] = mc_ext[pl.ds(2 * MRIM, 128)].astype(HALF)
+    mcot[pl.ds(192, MRIM)] = (mc_ext[pl.ds(256, MRIM)] + mesh_rim[1]).astype(HALF)
+    lat[...] = dot(mcot[...], w_msend[...], ((1,), (1,)))
+    gain_rows[...] = jnp.zeros_like(gain_rows)
+
+    def unnormalise(step, total):
+        rows = rows_at(step, 16)
+        flat = normed[rows]
+        product = lat[rows] * flat
+        scaled = lat[rows] * gain[...].astype(FULL)
+        mean = jnp.mean(scaled * flat, axis=-1, keepdims=True)
+        ucot[rows] = ((scaled - flat * mean) * inv[rows][:, :1]).astype(HALF)
+        return total + product[:8] + product[8:]
+
+    gain_total = lax.fori_loop(0, 16, unnormalise, jnp.zeros((8, 512), FULL))
+    gain_sum = jnp.sum(gain_total, axis=0, keepdims=True)
+    for part in range(4):
+        gain_rows[part : part + 1, :] = gain_sum[:, 128 * part : 128 * part + 128]
+    acot[...] = dot(ucot[...], w_update[...], ((1,), (1,))) * 0.5
+
+    def encode_back(number):
+        for part in range(NODES // 16):
+            rows = pl.ds(pl.multiple_of(number * NODES + part * 16, 16), 16)
+            cotangent = acot[rows]
+            total = jnp.zeros((16, 512), FULL)
+            for k in range(KE):
+                at = k * NODES + part * 16
+                piece = cotangent * slope[number, at : at + 16].astype(FULL)
+                total = total + piece
+                ecot[number, at : at + 16] = piece.astype(HALF)
+            rsum[rows] = total.astype(HALF)
+
+    def scatter(tile, numbers):
+        total = None
+        for number in numbers:
+            lines = lax.broadcasted_iota(jnp.int32, (256, DEPTH), 0) + tile * 256
+            selector = jnp.where(enc_row[number] == lines, 1.0, 0.0).astype(HALF)
+            piece = dot(selector, ecot[number])
+            total = piece if total is None else total + piece
+        return total
+
+    loop(2, lambda step: encode_back(step * 7))
+    rim_out[0] = scatter(0, (0,)).astype(HALF)
+    rim_out[1] = scatter(9, (7,)).astype(HALF)
+    grid_back = exchange(6, rim_out.at[0], rim_in.at[1], rim_out.at[1], rim_in.at[0])
+    loop(7, encode_back, 1)
+    edge[0] = scatter(1, (0, 1))
+    edge[1] = scatter(8, (6, 7))
+
+    def inner_tile(tile):
+        scot[pl.ds(pl.multiple_of((tile - 1) * 256, 256), 256)] = scatter(
+            tile, (tile - 2, tile - 1, tile)
+        ).astype(HALF)
+
+    loop(8, inner_tile, 2)
+    contract(0, mesh, rsum, 1, 256)
+    contract(2, agg, ucot, 1, 256)
+    contract(3, mlat, mcot, 1, 256)
+    mesh_grad[...] = (lat[...] + dot(rsum[...], w_recv[...], ((1,), (1,)))).astype(HALF)
+    for copy in grid_back:
+        copy.wait_recv()
+    scot[pl.ds(0, GRIM)] = (edge[0] + rim_in[0].astype(FULL)).astype(HALF)
+    scot[pl.ds(2048 - GRIM, GRIM)] = (edge[1] + rim_in[1].astype(FULL)).astype(HALF)
+    contract(1, grid, scot, 4, 512)
+
+    def last_part(step):
+        rows = rows_at(step, 512)
+        grid_grad[rows] = (gp[rows] + dot(scot[rows], w_send[...], ((1,), (1,)))).astype(HALF)
+
+    loop(4, last_part)
+    for copy in sent:
+        copy.wait_send()
+
+
+def local_work(*operands):
+    vmem = pltpu.VMEM
+    return pl.pallas_call(
+        local_kernel,
+        out_shape=(
+            jax.ShapeDtypeStruct((2048, 512), HALF),
+            jax.ShapeDtypeStruct((256, 512), HALF),
+            jax.ShapeDtypeStruct((6, 512, 512), HALF),
+            jax.ShapeDtypeStruct((8, 128), FULL),
+        ),
+        in_specs=[pl.BlockSpec(memory_space=vmem)] * len(operands),
+        out_specs=[pl.BlockSpec(memory_space=vmem)] * 4,
+        scratch_shapes=[
+            vmem((2048 + 2 * GRIM, 512), HALF),
+            vmem((2048, 512), FULL),
+            vmem((2048, 512), FULL),
+            vmem((256, 512), FULL),
+            vmem((3 * CELLS, 512), FULL),
+            vmem((8, DEPTH, 512), HALF),
+            vmem((256, 512), HALF),
+            vmem((256, 512), FULL),
+            vmem((256, 128), FULL),
+            vmem((256, 512), HALF),
+            vmem((256 + 2 * MRIM, 512), HALF),
+            vmem((3, CELLS, 512), HALF),
+            vmem((2048, 512), HALF),
+            vmem((2048, 512), HALF),
+            vmem((256 + 2 * MRIM, 512), FULL),
+            vmem((2, MRIM, 512), FULL),
+            vmem((256, 512), FULL),
+            vmem((256, 512), HALF),
+            vmem((256, 512), HALF),
+            vmem((256, 512), FULL),
+            vmem((8, DEPTH, 512), HALF),
+            vmem((256, 512), HALF),
+            vmem((2048, 512), HALF),
+            vmem((2, GRIM, 512), HALF),
+            vmem((2, GRIM, 512), HALF),
+            vmem((2, GRIM, 512), FULL),
+            vmem((512, 512), FULL),
+            pltpu.SemaphoreType.DMA((8, 2)),
+        ],
+        compiler_params=pltpu.CompilerParams(
+            collective_id=1, has_side_effects=True, vmem_limit_bytes=60 * 1024 * 1024
+        ),
+    )(*operands)
+
+
 def shards(
     grid_latent,
     mesh_init,
@@ -336,90 +575,33 @@
     output_weight,
 ):
     band_index = lax.axis_index("graph")
-    grid_in = grid_latent[0]
-    mesh_in = mesh_init[0]
-    grid_cot = cotangent[0]
-    grid_rows = grid_in.shape[0]
-    mesh_rows = mesh_in.shape[0]
-    ratio_rows = grid_rows // mesh_rows
-    enc_block = min(mesh_rows, 128)
-    enc_width = enc_block * ratio_rows + 2 * GRIM
-    dec_block = min(grid_rows, 512)
-    dec_width = dec_block // ratio_rows + 2 * MRIM
-    send_proj = jnp.dot(grid_in, send_weight, preferred_element_type=jnp.float32).astype(
-        jnp.bfloat16
-    )
-    send_ext = neighbour_rows(send_proj, GRIM)
-    recv_proj = jnp.dot(mesh_in, recv_weight, preferred_element_type=jnp.float32).astype(
-        jnp.bfloat16
-    )
-    local_index = enc_senders - (band_index * grid_rows - GRIM)
-    live_mask = (jnp.arange(KE, dtype=jnp.int32)[:, None] < enc_counts[None, :]).astype(jnp.float32)
-    agg_total, deriv_all = slot_forward(
-        window_take(send_ext, local_index, enc_block, ratio_rows, 1, enc_width),
-        recv_proj,
-        live_mask,
-    )
-    aggregate = agg_total.astype(jnp.bfloat16)
-    update = jnp.dot(aggregate, update_weight, preferred_element_type=jnp.float32)
-    inv_rms = lax.rsqrt(jnp.mean(update * update, axis=-1, keepdims=True) + 1e-06)
-    normed = update * inv_rms
-    mesh_latent = (mesh_in.astype(jnp.float32) + norm_gain.astype(jnp.float32) * normed).astype(
-        jnp.bfloat16
-    )
-    mesh_proj = jnp.dot(mesh_latent, mesh_send_weight, preferred_element_type=jnp.float32).astype(
-        jnp.bfloat16
-    )
-    mesh_ext = neighbour_rows(mesh_proj, MRIM)
-    dec_index = dec_senders - (band_index * mesh_rows - MRIM)
-    grid_proj = jnp.dot(grid_in, grid_recv_weight, preferred_element_type=jnp.float32)
-    dec_rows = window_take(mesh_ext, dec_index, dec_block, 1, ratio_rows, dec_width)
-    dec_pre = dec_rows.astype(jnp.float32) + grid_proj[None]
-    dec_value, dec_slope = activation(dec_pre)
-    dec_sum = jnp.sum(dec_value, axis=0).astype(jnp.bfloat16)
-    out_term = dot_rows(dec_sum, grid_cot)
-    sum_cot = dot_cols(grid_cot, output_weight)
-    dec_narrow = lax.optimization_barrier((sum_cot[None] * dec_slope).astype(jnp.bfloat16))
-    recv_cot = jnp.sum(dec_narrow.astype(jnp.float32), axis=0).astype(jnp.bfloat16)
-    mesh_cot_ext = window_add(
-        mesh_rows + 2 * MRIM, dec_index, dec_narrow, dec_block, 1, ratio_rows, dec_width
-    )
-    mesh_cot = return_rims(mesh_cot_ext, MRIM).astype(jnp.bfloat16)
-    grecv_term = dot_rows(grid_in, recv_cot)
-    msend_term = dot_rows(mesh_latent, mesh_cot)
-    latent_cot = dot_cols(mesh_cot, mesh_send_weight)
-    gain_term = jnp.sum(latent_cot * normed, axis=0)
-    normed_cot = latent_cot * norm_gain.astype(jnp.float32)
-    update_cot = (
-        (normed_cot - normed * jnp.mean(normed_cot * normed, axis=-1, keepdims=True)) * inv_rms
-    ).astype(jnp.bfloat16)
-    update_term = dot_rows(aggregate, update_cot)
-    agg_cot = dot_cols(update_cot, update_weight)
-    enc_cot = (agg_cot[None] * deriv_all).astype(jnp.bfloat16)
-    enc_cot = lax.optimization_barrier(enc_cot)
-    recv_sum = jnp.sum(enc_cot.astype(jnp.float32), axis=0).astype(jnp.bfloat16)
-    send_cot_ext = window_add(
-        grid_rows + 2 * GRIM, local_index, enc_cot, enc_block, ratio_rows, 1, enc_width
-    )
-    send_cot = return_rims(send_cot_ext, GRIM).astype(jnp.bfloat16)
-    recv_term = dot_rows(mesh_in, recv_sum)
-    send_term = dot_rows(grid_in, send_cot)
-    mesh_grad = (latent_cot + dot_cols(recv_sum, recv_weight)).astype(jnp.bfloat16)[None]
-    grid_total = (
-        grid_cot.astype(jnp.float32)
-        + dot_cols(recv_cot, grid_recv_weight)
-        + dot_cols(send_cot, send_weight)
-    )
-    grid_grad = grid_total.astype(jnp.bfloat16)[None]
-    terms = (recv_term, send_term, update_term, msend_term, grecv_term, out_term)
-    stacked = jnp.stack([term.astype(jnp.bfloat16) for term in terms])
-    gain_rows = jnp.concatenate([gain_term.reshape(4, 128), jnp.zeros((4, 128), jnp.float32)])
+    enc_index = enc_senders - (band_index * 2048 - GRIM)
+    dec_index = dec_senders - (band_index * 256 - MRIM)
+    enc_row = enc_index.reshape(KE, 8, NODES).transpose(1, 0, 2).reshape(8, 1, DEPTH)
+    dec_row = dec_index.reshape(3, 4, 1, CELLS)
+    grid_grad, mesh_grad, stacked, gain_rows = local_work(
+        grid_latent[0],
+        mesh_init[0],
+        cotangent[0],
+        enc_index.T,
+        enc_row,
+        enc_counts.reshape(256, 1),
+        dec_index.T,
+        dec_row,
+        recv_weight,
+        send_weight,
+        update_weight,
+        norm_gain.reshape(1, 512),
+        mesh_send_weight,
+        grid_recv_weight,
+        output_weight,
+    )
     totals, gain_total = sum_everywhere(stacked, gain_rows)
-    totals = totals.astype(jnp.float32)
-    factor = 1.0 / math.sqrt(grid_rows * lax.axis_size("graph") * lax.axis_size("dp"))
+    totals = totals.astype(FULL)
+    factor = 1.0 / math.sqrt(2048 * lax.axis_size("graph") * lax.axis_size("dp"))
     return (
-        grid_grad,
-        mesh_grad,
+        grid_grad[None],
+        mesh_grad[None],
         totals[0] * factor,
         totals[1] * factor,
         totals[2] * factor,

time: 282 us -> 117 us (0.41)
  matrix products: 66.6 us -> 0 us
  other arithmetic: 67.3 us -> 6.01 us
  Pallas kernels: 63.1 us -> 101 us
  local copies, waits for them, and re-layouts: 43 us -> 9.23 us
  starting transfers between devices: 23.3 us -> 0 us
  loops' own time: 10.9 us -> 0 us
  waiting for transfers between devices: 4.75 us -> 0 us
    dot_general x29 -> x0, matrix products: 66.6 us -> none  [the longest x6 19.3 us: one_block(): jnp.einsum('smw,smd->wd', selector, part_values, preferred_element_type=j...]
    pallas_call x0 -> x1, Pallas kernels: none -> 58.1 us  [local_work(): pl.pallas_call(local_kernel, out_shape=(jax.ShapeDtypeStruct((2048, 512),...]
    convert_element_type x10 -> x1, other arithmetic: 30 us -> 0.88 us  [shards(): totals = totals.astype(FULL)]
    ppermute x8 -> x0, starting transfers between devices: 23.3 us -> none  [the longest x4 17.5 us: with_halo(): lax.ppermute(lax.slice_in_dim(block, block.shape[dim] - width, None, axis...]
    pallas_call x1, Pallas kernels: 63.1 us -> 42.9 us  [sum_everywhere(): pl.pallas_call(sum_kernel, out_shape=(jax.ShapeDtypeStruct((6, 512, 512),...]
    reduce_sum x4 -> x0, other arithmetic: 19.9 us -> none  [the longest x1 8.18 us: shards(): dec_sum = jnp.sum(dec_value, axis=0).astype(jnp.bfloat16)]
    convert_element_type x2 -> x0, local copies, waits for them, and re-layouts: 14.2 us -> none  [the longest x1 10.8 us: shards(): dec_pre = dec_rows.astype(jnp.float32) + grid_proj[None]]
    another operation x4 -> x0, loops' own time: 10.9 us -> none  [the longest x2 5.48 us: window_add(): lax.scan(one_block, start_totals, jnp.arange(blocks, dtype=jnp.int32))]
  transfers between devices with their start and end apart: 8 -> 0, of which waited for: 1 -> 0; matrix products, arithmetic and copies ran while one was open for 16% -> 0% of each run, Pallas kernels for 0% -> 0%
where the time goes in v2:
time: 117 us
  Pallas kernels  101 us (86%)
  local copies, waits for them, and re-layouts  9.23 us (8%)
  other arithmetic  6.01 us (5%)
    pallas_call x1, Pallas kernels, local_work(): pl.pallas_call(local_kernel, out_shape=(jax.ShapeDtypeStruct((2048, 512),...  58.1 us
    pallas_call x1, Pallas kernels, sum_everywhere(): pl.pallas_call(sum_kernel, out_shape=(jax.ShapeDtypeStruct((6, 512, 512),...  42.9 us
    unnamed x10, local copies, waits for them, and re-layouts  4.75 us
    mul x1, other arithmetic, shards(): totals[5] * factor  2.76 us

profile of v2, /device:TPU:1, one launch (start us, length us, event | category | flops | bytes accessed | tf_op | source)
XLA Modules:
  0.0 116.9 jit_solution(3146620154178356509)
XLA Ops:
  0.6 1.3 %reshape.52.gain = bf16[1,512]{1,0:T(2,128)(2,1)} reshape(bf16[512]{0:T(512)(128)(2,1)} %param.22) | data formatting | bytes 2048 | tf_op jit(solution)/shard_map/reshape | solution.py:594
  1.9 0.8 copy.32
  2.7 0.7 fusion.7.enc_col
  3.4 0.1 copy.33
  3.5 0.7 reshape.53.enc_row
  4.2 1.5 %copy.38.counts = s32[256,1]{1,0:T(8,128)} copy(s32[256,1]{0,1:T(1,128)} %bitcast.35) | data formatting | bytes 2048 | tf_op jit(solution)/shard_map/reshape | solution.py:588
  5.7 1.1 copy.34
  6.8 1.0 fusion.6.dec_col
  7.9 0.1 broadcast_subtract_fusion
  7.9 0.9 copy.39.dec_row
  8.9 58.1 %shard_map.196 = (bf16[2048,512]{1,0:T(8,128)(2,1)}, bf16[256,512]{1,0:T(8,128)(2,1)}, bf16[6,512,512]{2,1,0:T(8,128)(2,1)}, f32[8,128]{1,0:T(8,128)}) custom-call(bf16[2048,512]{1,0:T(8,128)(2,1)} %bitcast.28, bf16[256,512]{1,0:T(8,128)(2,1)} %bitcast.32, bf16[2048,512]{1,0:T(8,128)(2,1)} %bitcast.29, s32[256,12]{1,0:T(8,128)} %fusion.7.enc_col, ...), custom_call_target="tpu_custom_call" | custom-call | tf_op jit(solution)/shard_map/pallas_call | solution.py:516
  67.0 0.0 copy-start
  67.0 0.7 copy-done
  67.6 42.9 %shard_map.197 = (bf16[6,512,512]{2,1,0:T(8,128)(2,1)S(1)}, f32[8,128]{1,0:T(8,128)S(1)}) custom-call(bf16[6,512,512]{2,1,0:T(8,128)(2,1)} %get-tuple-element.17.grads, f32[8,128]{1,0:T(8,128)S(1)} %copy-done), custom_call_target="tpu_custom_call" | custom-call | tf_op jit(solution)/shard_map/pallas_call | solution.py:207
  110.5 0.6 multiply_bitcast_fusion
  111.1 0.9 convert_element_type.3
  112.0 0.0 copy-start.1
  112.0 2.8 %fusion = (f32[512,512]{1,0:T(8,128)}, f32[512,512]{1,0:T(8,128)}, f32[512,512]{1,0:T(8,128)}, f32[512,512]{1,0:T(8,128)}, f32[512,512]{1,0:T(8,128)}, /*index=5*/f32[512,512]{1,0:T(8,128)}) fusion(f32[6,512,512]{2,1,0:T(8,128)S(1)} %convert_element_type.3), kind=kLoop, calls=%fused_computation.1 | loop fusion | flops 1572864 | bytes 12582912 | tf_op jit(solution)/shard_map/mul | solution.py:611
  114.8 0.0 copy-start.2
  114.8 0.1 copy-done.1
  114.9 1.3 %copy.42 = bf16[1,2048,512]{2,1,0:T(8,128)(2,1)} copy(bf16[1,2048,512]{2,1,0:T(8,128)(2,1)S(1)} %bitcast.30) | data formatting | bytes 4194304
  116.2 0.0 copy-done.2
  116.2 0.7 copy.43
  (1 shorter events, 0.0 us)
Async XLA Ops:
  67.0 0.7 copy-start
  112.0 2.9 %copy-start.1 = (bf16[2048,512]{1,0:T(8,128)(2,1)S(1)}, bf16[2048,512]{1,0:T(8,128)(2,1)}, u32[]{:S(2)}) copy-start(bf16[2048,512]{1,0:T(8,128)(2,1)} %get-tuple-element.15) | copy-start | bytes 6291460
  114.8 1.4 %copy-start.2 = (bf16[256,512]{1,0:T(8,128)(2,1)S(1)}, bf16[256,512]{1,0:T(8,128)(2,1)}, u32[]{:S(2)}) copy-start(bf16[256,512]{1,0:T(8,128)(2,1)} %get-tuple-element.16) | copy-start | bytes 786436

commit v3 on v2

v3 whole, which is shorter than its diff:
```python
import math

import jax
import jax.numpy as jnp
from jax import lax
from jax.experimental import pallas as pl
from jax.experimental.pallas import tpu as pltpu
from jax.sharding import PartitionSpec as P

KE = 12
GRIM = 256
MRIM = 64


STRIDES = (16, 4, 1)
ORDERS = ((0, 1, 2), (1, 2, 0), (2, 0, 1))


def remote(src, dst, sems, target):
    return pltpu.make_async_remote_copy(
        src_ref=src,
        dst_ref=dst,
        send_sem=sems.at[0],
        recv_sem=sems.at[1],
        device_id=target,
        device_id_type=pl.DeviceIdType.MESH,
    )


HALF = jnp.bfloat16
FULL = jnp.float32
NODES = 32
DEPTH = KE * NODES
REACH = NODES * 8 + 2 * GRIM
CELLS = 512
SPAN = CELLS // 8 + 2 * MRIM
PARTS = ((0, 256), (256, 128), (384, 128))


def dot(left, right, dims=((1,), (0,))):
    return lax.dot_general(left, right, (dims, ((), ())), preferred_element_type=FULL)


def loop(count, body, start=0):
    lax.fori_loop(start, count, lambda step, carry: (body(step), carry)[1], 0)


def rows_at(index, size):
    return pl.ds(pl.multiple_of(index * size, size), size)


def half_silu(half_pre):
    bend = jnp.tanh(half_pre)
    lifted = 1.0 + bend
    value = half_pre * lifted
    return value, lifted + value * (1.0 - bend)


def whole_kernel(
    grid_any, mesh_any, cot_any, enc, counts, dec,
    w_recv_any, w_send_any, w_update_any, gain, w_msend_any, w_grecv_any, w_out_any,
    grid_grad, mesh_grad, totals, gain_total,
    grid_ext, mesh, cot, w_recv, w_send, w_update, w_msend, w_grecv, w_out,
    stage, enc_col, enc_row, dec_stage, dec_col,
    send_ext, gp, sc, rp, taken, slope, agg, normed, inv, mlat, mesh_ext,
    dcot, dsum, rcot, mc_ext, mesh_rim, lat, mcot, ucot, acot, rsum,
    scot, rim_in, acc, mgrad,
    terms, pair_in, paired, r1, s2, r2, r3, summed, gain_in, gain_held,
    load_sem, store_sem, sems, pair_sem, rs_sem, ag_sem, last_sem, gain_sem,
):
    core = lax.axis_index("dp")
    place = lax.axis_index("graph")
    twin = {"dp": 1 - core}
    left = {"graph": lax.rem(place + 63, 64)}
    right = {"graph": lax.rem(place + 1, 64)}
    coords = [lax.rem(place // stride, 4) for stride in STRIDES]

    def peer(axis, offset):
        moved = lax.rem(coords[axis] + offset, 4)
        return moved, {"graph": place + (moved - coords[axis]) * STRIDES[axis]}

    loads = {}
    for number, (name, source, target) in enumerate((
        ("w_send", w_send_any, w_send),
        ("grid", grid_any, grid_ext.at[pl.ds(GRIM, 2048)]),
        ("mesh", mesh_any, mesh),
        ("w_recv", w_recv_any, w_recv),
        ("w_grecv", w_grecv_any, w_grecv),
        ("cot", cot_any, cot),
        ("w_out", w_out_any, w_out),
        ("w_update", w_update_any, w_update),
        ("w_msend", w_msend_any, w_msend),
    )):
        loads[name] = pltpu.make_async_copy(source, target, load_sem.at[number])
        loads[name].start()

    barrier = pltpu.get_barrier_semaphore()
    targets = [left, right, twin]
    targets += [peer(axis, offset)[1] for axis in range(3) for offset in (1, 2, 3)]
    for target in targets:
        pl.semaphore_signal(
            barrier, inc=1, device_id=target, device_id_type=pl.DeviceIdType.MESH
        )
    pl.semaphore_wait(barrier, 12)
    sent = []

    def exchange(index, low, low_target, high, high_target):
        pair = [
            remote(low, low_target, sems.at[index], left),
            remote(high, high_target, sems.at[index + 1], right),
        ]
        for copy in pair:
            copy.start()
        sent.extend(pair)
        return pair

    grid_halo = exchange(
        0,
        grid_any.at[pl.ds(0, GRIM)],
        grid_ext.at[pl.ds(2048 + GRIM, GRIM)],
        grid_any.at[pl.ds(2048 - GRIM, GRIM)],
        grid_ext.at[pl.ds(0, GRIM)],
    )

    stage[...] = jnp.zeros_like(stage)
    stage[0:KE] = enc[...] - (place * 2048 - GRIM)
    stage[KE : KE + 1] = counts[...].reshape(1, 256)
    enc_col[...] = jnp.transpose(stage[...])
    for number in range(8):
        for k in range(KE):
            enc_row[number, :, k * NODES : (k + 1) * NODES] = stage[
                k : k + 1, number * NODES : (number + 1) * NODES
            ]
    dec_stage[...] = jnp.zeros_like(dec_stage)
    dec_stage[0:3] = dec[...] - (place * 256 - MRIM)
    dec_col[...] = jnp.transpose(dec_stage[...])

    def project(start, size):
        rows = pl.ds(start, size)
        send_ext[rows] = (dot(grid_ext[rows], w_send[...]) * 0.5).astype(HALF)

    loads["w_send"].wait()
    loads["grid"].wait()
    loop(4, lambda step: project(pl.multiple_of(GRIM + step * 512, 256), 512))
    loads["mesh"].wait()
    loads["w_recv"].wait()
    rp[...] = dot(mesh[...], w_recv[...]).astype(HALF).astype(FULL) * 0.5
    loads["w_grecv"].wait()
    loads["cot"].wait()
    loads["w_out"].wait()

    def dense(step):
        rows = rows_at(step, 512)
        shifted = pl.ds(pl.multiple_of(GRIM + step * 512, 256), 512)
        gp[rows] = dot(grid_ext[shifted], w_grecv[...]) * 0.5
        sc[rows] = dot(cot[rows], w_out[...], ((1,), (1,))) * 0.5

    loop(4, dense)

    def encode(number):
        columns = lax.broadcasted_iota(jnp.int32, (NODES, REACH), 1) + number * (NODES * 8)
        picks = enc_col[rows_at(number, NODES)]
        selector = jnp.concatenate(
            [
                jnp.where(picks[:, k : k + 1] == columns, 1.0, 0.0).astype(HALF)
                for k in range(KE)
            ]
        )
        taken[pl.ds(0, DEPTH)] = dot(
            selector, send_ext[pl.ds(pl.multiple_of(number * (NODES * 8), 256), REACH)]
        )
        for part in range(NODES // 16):
            rows = pl.ds(pl.multiple_of(number * NODES + part * 16, 16), 16)
            number_live = enc_col[rows][:, KE : KE + 1]
            receiver = rp[rows]
            total = jnp.zeros((16, 512), FULL)
            for k in range(KE):
                at = k * NODES + part * 16
                value, bend = half_silu(taken[at : at + 16] + receiver)
                mask = jnp.where(number_live > k, 1.0, 0.0)
                total = total + value * mask
                slope[number, at : at + 16] = (bend * mask).astype(HALF)
            agg[rows] = total.astype(HALF)

    loop(7, encode, 1)
    for copy in grid_halo:
        copy.wait_recv()
    project(0, GRIM)
    project(2048 + GRIM, GRIM)
    loop(2, lambda step: encode(step * 7))

    loads["w_update"].wait()
    acot[...] = dot(agg[...], w_update[...])
    wide_gain = gain[...].astype(FULL).reshape(1, 512)

    def normalise(step):
        rows = rows_at(step, 16)
        update = acot[rows]
        scale = lax.rsqrt(jnp.mean(update * update, axis=-1, keepdims=True) + 1e-06)
        inv[rows] = jnp.broadcast_to(scale, (16, 128))
        flat = update * scale
        normed[rows] = flat
        mlat[rows] = (mesh[rows].astype(FULL) + wide_gain * flat).astype(HALF)

    loop(16, normalise)
    loads["w_msend"].wait()
    mesh_ext[pl.ds(MRIM, 256)] = (dot(mlat[...], w_msend[...]) * 0.5).astype(HALF)
    mesh_halo = exchange(
        2,
        mesh_ext.at[pl.ds(MRIM, MRIM)],
        mesh_ext.at[pl.ds(256 + MRIM, MRIM)],
        mesh_ext.at[pl.ds(256, MRIM)],
        mesh_ext.at[pl.ds(0, MRIM)],
    )
    mc_ext[...] = jnp.zeros_like(mc_ext)

    def decode(number):
        base = pl.multiple_of(number * (CELLS // 8), 64)
        cells = rows_at(number, CELLS)
        window = mesh_ext[pl.ds(base, SPAN)]
        columns = lax.broadcasted_iota(jnp.int32, (CELLS, SPAN), 1) + base
        picks = dec_col[cells]
        for j in range(3):
            selector = jnp.where(picks[:, j : j + 1] == columns, 1.0, 0.0).astype(HALF)
            taken[pl.ds(j * CELLS, CELLS)] = dot(selector, window)

        def cell_rows(step):
            inner = rows_at(step, 16)
            rows = pl.ds(pl.multiple_of(number * CELLS + step * 16, 16), 16)
            own = gp[rows]
            cotangent = sc[rows]
            total = jnp.zeros((16, 512), FULL)
            back = jnp.zeros((16, 512), FULL)
            for j in range(3):
                value, bend = half_silu(
                    taken[pl.ds(pl.multiple_of(j * CELLS + step * 16, 16), 16)] + own
                )
                total = total + value
                part = cotangent * bend
                back = back + part
                dcot[j, inner] = part.astype(HALF)
            dsum[rows] = total.astype(HALF)
            rcot[rows] = back.astype(HALF)

        lax.fori_loop(0, CELLS // 16, lambda i, c: (cell_rows(i), c)[1], 0, unroll=4)
        lines = lax.broadcasted_iota(jnp.int32, (SPAN, CELLS), 0) + base
        added = mc_ext[pl.ds(base, SPAN)]
        for j in range(3):
            line = dec_stage[j : j + 1, pl.ds(pl.multiple_of(number * CELLS, CELLS), CELLS)]
            selector = jnp.where(line == lines, 1.0, 0.0).astype(HALF)
            added = added + dot(selector, dcot[j])
        mc_ext[pl.ds(base, SPAN)] = added

    loop(3, decode, 1)
    for copy in mesh_halo:
        copy.wait_recv()
    loop(2, lambda step: decode(step * 3))
    mesh_back = exchange(
        4,
        mc_ext.at[pl.ds(0, MRIM)],
        mesh_rim.at[1],
        mc_ext.at[pl.ds(256 + MRIM, MRIM)],
        mesh_rim.at[0],
    )

    def contract(slot, lefts, rights, count, size, shift=0):
        acc[...] = jnp.zeros_like(acc)

        def piece(step):
            rows = rows_at(step, size)
            moved = pl.ds(pl.multiple_of(step * size + shift, 256), size)
            acc[...] += dot(lefts[moved], rights[rows], ((0,), (0,)))

        loop(count, piece)
        terms[slot] = acc[...].astype(HALF)

    def fan(source, target, semaphores, axis):
        copies = []
        for offset in (1, 2, 3):
            moved, device = peer(axis, offset)
            copy = remote(source(moved), target(offset), semaphores.at[offset - 1], device)
            copy.start()
            copies.append(copy)
        sent.extend(copies)
        return copies

    def everywhere(group):
        own = 2 * group + core
        copy = remote(
            terms.at[2 * group + 1 - core], pair_in.at[group], pair_sem.at[group], twin
        )
        copy.start()
        sent.append(copy)
        yield
        copy.wait_recv()
        paired[group] = (terms[own].astype(FULL) + pair_in[group].astype(FULL)).astype(HALF)
        orders = [ORDERS[(p + group) % 3] for p in range(3)]
        columns = [pl.ds(*PARTS[p]) for p in range(3)]
        waves = [
            fan(
                lambda moved: paired.at[group, rows_at(moved, 128), columns[p]],
                lambda offset: r1.at[group, offset - 1, :, columns[p]],
                rs_sem.at[3 * group + p],
                orders[p][0],
            )
            for p in range(3)
        ]
        yield
        for p in range(3):
            for copy in waves[p]:
                copy.wait_recv()
            total = paired[group, rows_at(coords[orders[p][0]], 128), columns[p]].astype(FULL)
            for slot in range(3):
                total = total + r1[group, slot, :, columns[p]].astype(FULL)
            s2[group, :, columns[p]] = total.astype(HALF)
            waves[p] = fan(
                lambda moved: s2.at[group, rows_at(moved, 32), columns[p]],
                lambda offset: r2.at[group, offset - 1, :, columns[p]],
                rs_sem.at[9 + 3 * group + p],
                orders[p][1],
            )
        yield
        for p in range(3):
            for copy in waves[p]:
                copy.wait_recv()
            total = s2[group, rows_at(coords[orders[p][1]], 32), columns[p]].astype(FULL)
            for slot in range(3):
                total = total + r2[group, slot, :, columns[p]].astype(FULL)
            mine = coords[orders[p][2]]
            r3[group, mine, :, columns[p]] = total.astype(HALF)
            waves[p] = fan(
                lambda moved: r3.at[group, mine, :, columns[p]],
                lambda offset: r3.at[group, mine, :, columns[p]],
                rs_sem.at[18 + 3 * group + p],
                orders[p][2],
            )
        yield
        for p in range(3):
            for copy in waves[p]:
                copy.wait_recv()
            total = r3[group, 0, :, columns[p]].astype(FULL)
            for slot in range(1, 4):
                total = total + r3[group, slot, :, columns[p]].astype(FULL)
            number = coords[orders[p][0]] * 4 + coords[orders[p][1]]
            rows = rows_at(number, 32)
            summed[own, rows, columns[p]] = total.astype(HALF)
            piece = summed.at[own, rows, columns[p]]
            waves[p] = fan(
                lambda moved: piece, lambda offset: piece, ag_sem.at[3 * group + p], orders[p][1]
            )
        yield
        for p in range(3):
            for copy in waves[p]:
                copy.wait_recv()
            piece = summed.at[own, rows_at(coords[orders[p][0]], 128), columns[p]]
            waves[p] = fan(
                lambda moved: piece,
                lambda offset: piece,
                ag_sem.at[9 + 3 * group + p],
                orders[p][0],
            )
        yield
        last = []
        for p in range(3):
            for copy in waves[p]:
                copy.wait_recv()
            piece = summed.at[own, :, columns[p]]
            copy = remote(piece, piece, last_sem.at[group, p], twin)
            copy.start()
            last.append(copy)
        sent.extend(last)
        yield
        for copy in last:
            copy.wait_recv()
        copy = pltpu.make_async_copy(
            summed.at[pl.ds(2 * group, 2)],
            totals.at[pl.ds(2 * group, 2)],
            store_sem.at[group],
        )
        copy.start()
        stores.append(copy)
        yield

    def gain_everywhere():
        copy = remote(gain_held.at[0, 0], gain_in, gain_sem.at[9], twin)
        copy.start()
        sent.append(copy)
        yield
        copy.wait_recv()
        total = gain_held[0, 0] + gain_in[...]
        for step in range(3):
            mine = coords[step]
            gain_held[step + 1, mine] = total
            copies = []
            for offset in (1, 2, 3):
                piece = gain_held.at[step + 1, mine]
                copy = remote(
                    piece, piece, gain_sem.at[3 * step + offset - 1], peer(step, offset)[1]
                )
                copy.start()
                copies.append(copy)
            sent.extend(copies)
            yield
            for copy in copies:
                copy.wait_recv()
            total = gain_held[step + 1, 0]
            for slot in range(1, 4):
                total = total + gain_held[step + 1, slot]
        gain_total[...] = total
        yield

    stores = []
    running = []

    def pump(*chosen):
        for chain in chosen:
            next(chain)

    contract(0, grid_ext, rcot, 4, 512, GRIM)
    contract(1, dsum, cot, 4, 512)
    first = everywhere(0)
    second = everywhere(1)
    third = everywhere(2)
    fourth = gain_everywhere()
    pump(first)

    for copy in mesh_back:
        copy.wait_recv()
    mcot[pl.ds(0, MRIM)] = (mc_ext[pl.ds(MRIM, MRIM)] + mesh_rim[0]).astype(HALF)
    mcot[pl.ds(MRIM, 128)] = mc_ext[pl.ds(2 * MRIM, 128)].astype(HALF)
    mcot[pl.ds(192, MRIM)] = (mc_ext[pl.ds(256, MRIM)] + mesh_rim[1]).astype(HALF)
    lat[...] = dot(mcot[...], w_msend[...], ((1,), (1,)))
    gain_held[0, 0] = jnp.zeros((8, 128), FULL)

    def unnormalise(step, total):
        rows = rows_at(step, 16)
        flat = normed[rows]
        product = lat[rows] * flat
        scaled = lat[rows] * wide_gain
        mean = jnp.mean(scaled * flat, axis=-1, keepdims=True)
        ucot[rows] = ((scaled - flat * mean) * inv[rows][:, :1]).astype(HALF)
        return total + product[:8] + product[8:]

    rowwise = lax.fori_loop(0, 16, unnormalise, jnp.zeros((8, 512), FULL))
    gain_sum = jnp.sum(rowwise, axis=0, keepdims=True)
    for part in range(4):
        gain_held[0, 0, part : part + 1, :] = gain_sum[:, 128 * part : 128 * part + 128]
    acot[...] = dot(ucot[...], w_update[...], ((1,), (1,))) * 0.5
    pump(first)
    contract(2, agg, ucot, 1, 256)
    contract(3, mlat, mcot, 1, 256)
    pump(second, fourth)

    def encode_back(number):
        for part in range(NODES // 16):
            rows = pl.ds(pl.multiple_of(number * NODES + part * 16, 16), 16)
            cotangent = acot[rows]
            total = jnp.zeros((16, 512), FULL)
            for k in range(KE):
                at = k * NODES + part * 16
                piece = cotangent * slope[number, at : at + 16].astype(FULL)
                total = total + piece
                slope[number, at : at + 16] = piece.astype(HALF)
            rsum[rows] = total.astype(HALF)

    def scatter(tile, numbers):
        total = None
        for number in numbers:
            lines = lax.broadcasted_iota(jnp.int32, (256, DEPTH), 0) + tile * 256
            selector = jnp.where(enc_row[number] == lines, 1.0, 0.0).astype(HALF)
            piece = dot(selector, slope[number])
            total = piece if total is None else total + piece
        scot[rows_at(tile, 256)] = total.astype(HALF)

    loop(2, lambda step: encode_back(step * 7))
    scatter(0, (0,))
    scatter(9, (7,))
    grid_back = exchange(
        6,
        scot.at[pl.ds(0, GRIM)],
        rim_in.at[1],
        scot.at[pl.ds(2048 + GRIM, GRIM)],
        rim_in.at[0],
    )
    pump(first, second, fourth)
    loop(7, encode_back, 1)
    pump(first)
    scatter(1, (0, 1))
    scatter(8, (6, 7))
    pump(second, fourth)
    loop(5, lambda tile: scatter(tile, (tile - 2, tile - 1, tile)), 2)
    pump(first, fourth)
    loop(8, lambda tile: scatter(tile, (tile - 2, tile - 1, tile)), 5)
    pump(first, second)
    contract(4, mesh, rsum, 1, 256)
    contract(5, grid_ext, scot, 5, 512)
    pump(third, first, second, fourth)
    mgrad[...] = (lat[...] + dot(rsum[...], w_recv[...], ((1,), (1,)))).astype(HALF)
    copy = pltpu.make_async_copy(mgrad, mesh_grad, store_sem.at[3])
    copy.start()
    stores.append(copy)
    pump(third)

    def first_part(step):
        rows = rows_at(step, 512)
        gp[rows] = cot[rows].astype(FULL) + dot(rcot[rows], w_grecv[...], ((1,), (1,)))

    loop(2, first_part)
    pump(first, second)
    loop(4, first_part, 2)
    pump(third)
    for copy in grid_back:
        copy.wait_recv()
    for rim, start in ((0, GRIM), (1, 2048)):
        rows = pl.ds(start, GRIM)
        scot[rows] = (scot[rows].astype(FULL) + rim_in[rim].astype(FULL)).astype(HALF)

    def last_part(step):
        rows = rows_at(step, 512)
        shifted = pl.ds(pl.multiple_of(GRIM + step * 512, 256), 512)
        dsum[rows] = (gp[rows] + dot(scot[shifted], w_send[...], ((1,), (1,)))).astype(HALF)

    loop(2, last_part)
    pump(third, second)
    loop(4, last_part, 2)
    copy = pltpu.make_async_copy(dsum, grid_grad, store_sem.at[4])
    copy.start()
    stores.append(copy)
    for chain in (third, second, first, fourth):
        for unused in chain:
            pass
    for copy in sent:
        copy.wait_send()
    for copy in stores:
        copy.wait()


def everything(*operands):
    vmem = pltpu.VMEM
    anywhere = pl.BlockSpec(memory_space=pl.ANY)
    near = pl.BlockSpec(memory_space=vmem)
    return pl.pallas_call(
        whole_kernel,
        out_shape=(
            jax.ShapeDtypeStruct((2048, 512), HALF),
            jax.ShapeDtypeStruct((256, 512), HALF),
            jax.ShapeDtypeStruct((6, 512, 512), HALF),
            jax.ShapeDtypeStruct((8, 128), FULL),
        ),
        in_specs=[anywhere] * 3 + [near] * 3 + [anywhere] * 3 + [near] + [anywhere] * 3,
        out_specs=[anywhere, anywhere, anywhere, near],
        scratch_shapes=[
            vmem((2048 + 2 * GRIM, 512), HALF),
            vmem((256, 512), HALF),
            vmem((2048, 512), HALF),
        ]
        + [vmem((512, 512), HALF)] * 6
        + [
            vmem((16, 256), jnp.int32),
            vmem((256, 16), jnp.int32),
            vmem((8, 1, DEPTH), jnp.int32),
            vmem((8, 2048), jnp.int32),
            vmem((2048, 8), jnp.int32),
            vmem((2048 + 2 * GRIM, 512), HALF),
            vmem((2048, 512), FULL),
            vmem((2048, 512), FULL),
            vmem((256, 512), FULL),
            vmem((3 * CELLS, 512), FULL),
            vmem((8, DEPTH, 512), HALF),
            vmem((256, 512), HALF),
            vmem((256, 512), FULL),
            vmem((256, 128), FULL),
            vmem((256, 512), HALF),
            vmem((256 + 2 * MRIM, 512), HALF),
            vmem((3, CELLS, 512), HALF),
            vmem((2048, 512), HALF),
            vmem((2048, 512), HALF),
            vmem((256 + 2 * MRIM, 512), FULL),
            vmem((2, MRIM, 512), FULL),
            vmem((256, 512), FULL),
            vmem((256, 512), HALF),
            vmem((256, 512), HALF),
            vmem((256, 512), FULL),
            vmem((256, 512), HALF),
            vmem((2048 + 2 * GRIM, 512), HALF),
            vmem((2, GRIM, 512), HALF),
            vmem((512, 512), FULL),
            vmem((256, 512), HALF),
            vmem((6, 512, 512), HALF),
            vmem((3, 512, 512), HALF),
            vmem((3, 512, 512), HALF),
            vmem((3, 3, 128, 512), HALF),
            vmem((3, 128, 512), HALF),
            vmem((3, 3, 32, 512), HALF),
            vmem((3, 4, 32, 512), HALF),
            vmem((6, 512, 512), HALF),
            vmem((8, 128), FULL),
            vmem((4, 4, 8, 128), FULL),
            pltpu.SemaphoreType.DMA((9,)),
            pltpu.SemaphoreType.DMA((5,)),
            pltpu.SemaphoreType.DMA((8, 2)),
            pltpu.SemaphoreType.DMA((3, 2)),
            pltpu.SemaphoreType.DMA((27, 3, 2)),
            pltpu.SemaphoreType.DMA((18, 3, 2)),
            pltpu.SemaphoreType.DMA((3, 3, 2)),
            pltpu.SemaphoreType.DMA((10, 2)),
        ],
        compiler_params=pltpu.CompilerParams(
            collective_id=0, has_side_effects=True, vmem_limit_bytes=62 * 1024 * 1024
        ),
    )(*operands)


def shards(
    grid_latent,
    mesh_init,
    cotangent,
    enc_senders,
    enc_counts,
    dec_senders,
    recv_weight,
    send_weight,
    update_weight,
    norm_gain,
    mesh_send_weight,
    grid_recv_weight,
    output_weight,
):
    grid_grad, mesh_grad, totals, gain_total = everything(
        grid_latent[0],
        mesh_init[0],
        cotangent[0],
        enc_senders,
        enc_counts,
        dec_senders,
        recv_weight,
        send_weight,
        update_weight,
        norm_gain,
        mesh_send_weight,
        grid_recv_weight,
        output_weight,
    )
    totals = totals.astype(FULL)
    factor = 1.0 / math.sqrt(2048 * lax.axis_size("graph") * lax.axis_size("dp"))
    return (
        grid_grad[None],
        mesh_grad[None],
        totals[4] * factor,
        totals[5] * factor,
        totals[2] * factor,
        gain_total[:4].reshape(512) * factor,
        totals[3] * factor,
        totals[0] * factor,
        totals[1] * factor,
    )


def solution(mesh):
    return jax.shard_map(
        shards,
        mesh=mesh,
        in_specs=(
            P("dp", "graph", None),
            P("dp", "graph", None),
            P("dp", "graph", None),
            P(None, "graph"),
            P("graph"),
            P(None, "graph"),
            P(),
            P(),
            P(),
            P(),
            P(),
            P(),
            P(),
        ),
        out_specs=(
            P("dp", "graph", None),
            P("dp", "graph", None),
            P(),
            P(),
            P(),
            P(),
            P(),
            P(),
            P(),
        ),
        check_vma=False,
    )
```

time: 117 us -> 109 us (0.932)
  local copies, waits for them, and re-layouts: 9.23 us -> 2.13 us
  Pallas kernels: 101 us -> 99.2 us
    reshape x5 -> x0, local copies, waits for them, and re-layouts: 4.49 us -> none  [the longest x1 1.47 us: shards(): enc_counts.reshape(256, 1)]
    unnamed x10 -> x6, local copies, waits for them, and re-layouts: 4.75 us -> 2.13 us
    convert_element_type x1, other arithmetic: 0.88 us -> 2.75 us  [shards(): totals = totals.astype(FULL)]
    pallas_call x2 -> x1, Pallas kernels: 101 us -> 99.2 us  [everything(): pl.pallas_call(whole_kernel, out_shape=(jax.ShapeDtypeStruct((2048, 512),...]
    transpose x2 -> x0, other arithmetic: 1.71 us -> none  [shards(): grid_grad, mesh_grad, stacked, gain_rows = local_work(grid_latent[0], mes...]
where the time goes in v3:
time: 109 us
  Pallas kernels  99.2 us (91%)
  other arithmetic  6.77 us (6%)
  local copies, waits for them, and re-layouts  2.13 us (2%)
    pallas_call x1, Pallas kernels, everything(): pl.pallas_call(whole_kernel, out_shape=(jax.ShapeDtypeStruct((2048, 512),...  99.2 us
    mul x1, other arithmetic, shards(): totals[1] * factor  2.76 us
    convert_element_type x1, other arithmetic, shards(): totals = totals.astype(FULL)  2.75 us

profile of v3, /device:TPU:1, one launch (start us, length us, event | category | flops | bytes accessed | tf_op | source)
XLA Modules:
  0.0 108.8 jit_solution(4619023801658639395)
XLA Ops:
  0.6 99.2 %shard_map.196 = (bf16[2048,512]{1,0:T(8,128)(2,1)}, bf16[256,512]{1,0:T(8,128)(2,1)}, bf16[6,512,512]{2,1,0:T(8,128)(2,1)}, f32[8,128]{1,0:T(8,128)}) custom-call(bf16[2048,512]{1,0:T(8,128)(2,1)} %bitcast.20, bf16[256,512]{1,0:T(8,128)(2,1)} %bitcast.22, bf16[2048,512]{1,0:T(8,128)(2,1)} %bitcast.21, s32[12,256]{1,0:T(8,128)} %enc.1, s32[256]{0:T(256)} %counts.1, ...), custom_call_target="tpu_custom_call" | custom-call | tf_op jit(solution)/shard_map/pallas_call | solution.py:542
  99.8 1.3 %multiply_bitcast_fusion = f32[512]{0:T(512)} fusion(f32[8,128]{1,0:T(8,128)} %get-tuple-element.16), kind=kLoop, calls=%fused_computation.12 | loop fusion | flops 512 | bytes 4096 | tf_op jit(solution)/shard_map/mul | solution.py:652
  101.1 2.8 %convert_element_type.3 = f32[6,512,512]{2,1,0:T(8,128)S(1)} convert(bf16[6,512,512]{2,1,0:T(8,128)(2,1)} %get-tuple-element.15) | non-fusion elementwise | flops 1572864 | bytes 9437184 | tf_op jit(solution)/shard_map/convert_element_type | solution.py:644
  103.9 0.0 copy-start
  103.9 2.8 %fusion = (f32[512,512]{1,0:T(8,128)}, f32[512,512]{1,0:T(8,128)}, f32[512,512]{1,0:T(8,128)}, f32[512,512]{1,0:T(8,128)}, f32[512,512]{1,0:T(8,128)}, /*index=5*/f32[512,512]{1,0:T(8,128)}) fusion(f32[6,512,512]{2,1,0:T(8,128)S(1)} %convert_element_type.3), kind=kLoop, calls=%fused_computation.1 | loop fusion | flops 1572864 | bytes 12582912 | tf_op jit(solution)/shard_map/mul | solution.py:655
  106.6 0.1 copy-done
  106.7 0.0 copy-start.1
  106.7 1.3 %copy.24 = bf16[1,2048,512]{2,1,0:T(8,128)(2,1)} copy(bf16[1,2048,512]{2,1,0:T(8,128)(2,1)S(1)} %bitcast.19) | data formatting | bytes 4194304
  108.0 0.0 copy-done.1
  108.1 0.7 copy.25
Async XLA Ops:
  103.9 2.9 %copy-start = (bf16[2048,512]{1,0:T(8,128)(2,1)S(1)}, bf16[2048,512]{1,0:T(8,128)(2,1)}, u32[]{:S(2)}) copy-start(bf16[2048,512]{1,0:T(8,128)(2,1)} %get-tuple-element.13) | copy-start | bytes 6291460
  106.7 1.3 %copy-start.1 = (bf16[256,512]{1,0:T(8,128)(2,1)S(1)}, bf16[256,512]{1,0:T(8,128)(2,1)}, u32[]{:S(2)}) copy-start(bf16[256,512]{1,0:T(8,128)(2,1)} %get-tuple-element.14) | copy-start | bytes 786436

commit v4 on v3

--- a/solution.py
+++ b/solution.py
@@ -1,3 +1,4 @@
+import functools
 import math
 
 import jax
@@ -34,7 +35,7 @@
 REACH = NODES * 8 + 2 * GRIM
 CELLS = 512
 SPAN = CELLS // 8 + 2 * MRIM
-PARTS = ((0, 256), (256, 128), (384, 128))
+PARTS = ((0, 128), (128, 128), (256, 128), (384, 128))
 
 
 def dot(left, right, dims=((1,), (0,))):
@@ -101,7 +102,6 @@
         pl.semaphore_signal(
             barrier, inc=1, device_id=target, device_id_type=pl.DeviceIdType.MESH
         )
-    pl.semaphore_wait(barrier, 12)
     sent = []
 
     def exchange(index, low, low_target, high, high_target):
@@ -113,14 +113,6 @@
             copy.start()
         sent.extend(pair)
         return pair
-
-    grid_halo = exchange(
-        0,
-        grid_any.at[pl.ds(0, GRIM)],
-        grid_ext.at[pl.ds(2048 + GRIM, GRIM)],
-        grid_any.at[pl.ds(2048 - GRIM, GRIM)],
-        grid_ext.at[pl.ds(0, GRIM)],
-    )
 
     stage[...] = jnp.zeros_like(stage)
     stage[0:KE] = enc[...] - (place * 2048 - GRIM)
@@ -142,6 +134,15 @@
     loads["w_send"].wait()
     loads["grid"].wait()
     loop(4, lambda step: project(pl.multiple_of(GRIM + step * 512, 256), 512))
+    pl.semaphore_wait(barrier, 12)
+    grid_halo = exchange(
+        0,
+        grid_ext.at[pl.ds(GRIM, GRIM)],
+        grid_ext.at[pl.ds(2048 + GRIM, GRIM)],
+        grid_ext.at[pl.ds(2048, GRIM)],
+        grid_ext.at[pl.ds(0, GRIM)],
+    )
+
     loads["mesh"].wait()
     loads["w_recv"].wait()
     rp[...] = dot(mesh[...], w_recv[...]).astype(HALF).astype(FULL) * 0.5
@@ -294,19 +295,19 @@
         yield
         copy.wait_recv()
         paired[group] = (terms[own].astype(FULL) + pair_in[group].astype(FULL)).astype(HALF)
-        orders = [ORDERS[(p + group) % 3] for p in range(3)]
-        columns = [pl.ds(*PARTS[p]) for p in range(3)]
+        orders = [ORDERS[(p + group) % 3] for p in range(4)]
+        columns = [pl.ds(*PARTS[p]) for p in range(4)]
         waves = [
             fan(
                 lambda moved: paired.at[group, rows_at(moved, 128), columns[p]],
                 lambda offset: r1.at[group, offset - 1, :, columns[p]],
-                rs_sem.at[3 * group + p],
+                rs_sem.at[4 * group + p],
                 orders[p][0],
             )
-            for p in range(3)
+            for p in range(4)
         ]
         yield
-        for p in range(3):
+        for p in range(4):
             for copy in waves[p]:
                 copy.wait_recv()
             total = paired[group, rows_at(coords[orders[p][0]], 128), columns[p]].astype(FULL)
@@ -316,11 +317,11 @@
             waves[p] = fan(
                 lambda moved: s2.at[group, rows_at(moved, 32), columns[p]],
                 lambda offset: r2.at[group, offset - 1, :, columns[p]],
-                rs_sem.at[9 + 3 * group + p],
+                rs_sem.at[12 + 4 * group + p],
                 orders[p][1],
             )
         yield
-        for p in range(3):
+        for p in range(4):
             for copy in waves[p]:
                 copy.wait_recv()
             total = s2[group, rows_at(coords[orders[p][1]], 32), columns[p]].astype(FULL)
@@ -331,11 +332,11 @@
             waves[p] = fan(
                 lambda moved: r3.at[group, mine, :, columns[p]],
                 lambda offset: r3.at[group, mine, :, columns[p]],
-                rs_sem.at[18 + 3 * group + p],
+                rs_sem.at[24 + 4 * group + p],
                 orders[p][2],
             )
         yield
-        for p in range(3):
+        for p in range(4):
             for copy in waves[p]:
                 copy.wait_recv()
             total = r3[group, 0, :, columns[p]].astype(FULL)
@@ -346,22 +347,22 @@
             summed[own, rows, columns[p]] = total.astype(HALF)
             piece = summed.at[own, rows, columns[p]]
             waves[p] = fan(
-                lambda moved: piece, lambda offset: piece, ag_sem.at[3 * group + p], orders[p][1]
+                lambda moved: piece, lambda offset: piece, ag_sem.at[4 * group + p], orders[p][1]
             )
         yield
-        for p in range(3):
+        for p in range(4):
             for copy in waves[p]:
                 copy.wait_recv()
             piece = summed.at[own, rows_at(coords[orders[p][0]], 128), columns[p]]
             waves[p] = fan(
                 lambda moved: piece,
                 lambda offset: piece,
-                ag_sem.at[9 + 3 * group + p],
+                ag_sem.at[12 + 4 * group + p],
                 orders[p][0],
             )
         yield
         last = []
-        for p in range(3):
+        for p in range(4):
             for copy in waves[p]:
                 copy.wait_recv()
             piece = summed.at[own, :, columns[p]]
@@ -424,6 +425,11 @@
     fourth = gain_everywhere()
     pump(first)
 
+    def first_part(step):
+        rows = rows_at(step, 512)
+        gp[rows] = cot[rows].astype(FULL) + dot(rcot[rows], w_grecv[...], ((1,), (1,)))
+
+    loop(4, first_part)
     for copy in mesh_back:
         copy.wait_recv()
     mcot[pl.ds(0, MRIM)] = (mc_ext[pl.ds(MRIM, MRIM)] + mesh_rim[0]).astype(HALF)
@@ -446,10 +452,9 @@
     for part in range(4):
         gain_held[0, 0, part : part + 1, :] = gain_sum[:, 128 * part : 128 * part + 128]
     acot[...] = dot(ucot[...], w_update[...], ((1,), (1,))) * 0.5
-    pump(first)
     contract(2, agg, ucot, 1, 256)
     contract(3, mlat, mcot, 1, 256)
-    pump(second, fourth)
+    pump(second, fourth, first)
 
     def encode_back(number):
         for part in range(NODES // 16):
@@ -482,33 +487,20 @@
         scot.at[pl.ds(2048 + GRIM, GRIM)],
         rim_in.at[0],
     )
-    pump(first, second, fourth)
     loop(7, encode_back, 1)
-    pump(first)
     scatter(1, (0, 1))
     scatter(8, (6, 7))
-    pump(second, fourth)
     loop(5, lambda tile: scatter(tile, (tile - 2, tile - 1, tile)), 2)
-    pump(first, fourth)
     loop(8, lambda tile: scatter(tile, (tile - 2, tile - 1, tile)), 5)
-    pump(first, second)
     contract(4, mesh, rsum, 1, 256)
     contract(5, grid_ext, scot, 5, 512)
-    pump(third, first, second, fourth)
+    pump(third)
     mgrad[...] = (lat[...] + dot(rsum[...], w_recv[...], ((1,), (1,)))).astype(HALF)
     copy = pltpu.make_async_copy(mgrad, mesh_grad, store_sem.at[3])
     copy.start()
     stores.append(copy)
-    pump(third)
-
-    def first_part(step):
-        rows = rows_at(step, 512)
-        gp[rows] = cot[rows].astype(FULL) + dot(rcot[rows], w_grecv[...], ((1,), (1,)))
-
-    loop(2, first_part)
-    pump(first, second)
-    loop(4, first_part, 2)
-    pump(third)
+    pump(fourth, first, second, third)
+
     for copy in grid_back:
         copy.wait_recv()
     for rim, start in ((0, GRIM), (1, 2048)):
@@ -520,15 +512,12 @@
         shifted = pl.ds(pl.multiple_of(GRIM + step * 512, 256), 512)
         dsum[rows] = (gp[rows] + dot(scot[shifted], w_send[...], ((1,), (1,)))).astype(HALF)
 
-    loop(2, last_part)
-    pump(third, second)
-    loop(4, last_part, 2)
+    loop(4, last_part)
     copy = pltpu.make_async_copy(dsum, grid_grad, store_sem.at[4])
     copy.start()
     stores.append(copy)
-    for chain in (third, second, first, fourth):
-        for unused in chain:
-            pass
+    for chain in (fourth, first, second, third) * 8:
+        next(chain, None)
     for copy in sent:
         copy.wait_send()
     for copy in stores:
@@ -600,15 +589,74 @@
             pltpu.SemaphoreType.DMA((5,)),
             pltpu.SemaphoreType.DMA((8, 2)),
             pltpu.SemaphoreType.DMA((3, 2)),
-            pltpu.SemaphoreType.DMA((27, 3, 2)),
-            pltpu.SemaphoreType.DMA((18, 3, 2)),
-            pltpu.SemaphoreType.DMA((3, 3, 2)),
+            pltpu.SemaphoreType.DMA((36, 3, 2)),
+            pltpu.SemaphoreType.DMA((24, 3, 2)),
+            pltpu.SemaphoreType.DMA((3, 4, 2)),
             pltpu.SemaphoreType.DMA((10, 2)),
         ],
         compiler_params=pltpu.CompilerParams(
             collective_id=0, has_side_effects=True, vmem_limit_bytes=62 * 1024 * 1024
         ),
     )(*operands)
+
+
+def finish_kernel(factor, grid_in, mesh_in, totals, gain, *rest):
+    grid_out, mesh_out = rest[:2]
+    outs = rest[2:8]
+    gain_out, held, wide, grid_held, mesh_held, in_sem, out_sem, copy_sem = rest[8:]
+    reads = []
+    for slot in range(6):
+        reads.append(pltpu.make_async_copy(totals.at[slot], held.at[slot], in_sem.at[slot]))
+        reads[slot].start()
+    near = [
+        pltpu.make_async_copy(grid_in, grid_held, copy_sem.at[0]),
+        pltpu.make_async_copy(mesh_in, mesh_held, copy_sem.at[1]),
+    ]
+    for copy in near:
+        copy.start()
+    copies = [
+        pltpu.make_async_copy(grid_held, grid_out, copy_sem.at[2]),
+        pltpu.make_async_copy(mesh_held, mesh_out, copy_sem.at[3]),
+    ]
+    for part in range(4):
+        gain_out[128 * part : 128 * part + 128] = gain[part] * factor
+    for slot in range(6):
+        reads[slot].wait()
+        wide[slot] = held[slot].astype(FULL) * factor
+        copies.append(pltpu.make_async_copy(wide.at[slot], outs[slot], out_sem.at[slot]))
+        copies[-1].start()
+    for number in range(2):
+        near[number].wait()
+        copies[number].start()
+    for copy in copies:
+        copy.wait()
+
+
+def finish(factor, grid_grad, mesh_grad, totals, gain_total):
+    vmem = pltpu.VMEM
+    anywhere = pl.BlockSpec(memory_space=pl.ANY)
+    near = pl.BlockSpec(memory_space=vmem)
+    return pl.pallas_call(
+        functools.partial(finish_kernel, factor),
+        out_shape=[
+            jax.ShapeDtypeStruct((2048, 512), HALF),
+            jax.ShapeDtypeStruct((256, 512), HALF),
+        ]
+        + [jax.ShapeDtypeStruct((512, 512), FULL)] * 6
+        + [jax.ShapeDtypeStruct((512,), FULL)],
+        in_specs=[anywhere] * 3 + [near],
+        out_specs=[anywhere] * 8 + [near],
+        scratch_shapes=[
+            vmem((6, 512, 512), HALF),
+            vmem((6, 512, 512), FULL),
+            vmem((2048, 512), HALF),
+            vmem((256, 512), HALF),
+            pltpu.SemaphoreType.DMA((6,)),
+            pltpu.SemaphoreType.DMA((6,)),
+            pltpu.SemaphoreType.DMA((4,)),
+        ],
+        compiler_params=pltpu.CompilerParams(vmem_limit_bytes=62 * 1024 * 1024),
+    )(grid_grad, mesh_grad, totals, gain_total)
 
 
 def shards(
@@ -641,19 +689,10 @@
         grid_recv_weight,
         output_weight,
     )
-    totals = totals.astype(FULL)
     factor = 1.0 / math.sqrt(2048 * lax.axis_size("graph") * lax.axis_size("dp"))
-    return (
-        grid_grad[None],
-        mesh_grad[None],
-        totals[4] * factor,
-        totals[5] * factor,
-        totals[2] * factor,
-        gain_total[:4].reshape(512) * factor,
-        totals[3] * factor,
-        totals[0] * factor,
-        totals[1] * factor,
-    )
+    outs = finish(factor, grid_grad, mesh_grad, totals, gain_total)
+    order = (6, 7, 4, 8, 5, 2, 3)
+    return (outs[0][None], outs[1][None]) + tuple(outs[number] for number in order)
 
 
 def solution(mesh):

time: 109 us -> 89.9 us (0.82)
  Pallas kernels: 99.2 us -> 88.9 us
  other arithmetic: 6.77 us -> 0 us
  local copies, waits for them, and re-layouts: 2.13 us -> 0 us
    pallas_call x1, Pallas kernels: 99.2 us -> 82.1 us  [everything(): pl.pallas_call(whole_kernel, out_shape=(jax.ShapeDtypeStruct((2048, 512),...]
    pallas_call x0 -> x1, Pallas kernels: none -> 6.79 us  [finish(): pl.pallas_call(functools.partial(finish_kernel, factor), out_shape=[jax.S...]
    mul x2 -> x0, other arithmetic: 4.02 us -> none  [the longest x1 2.76 us: shards(): totals[1] * factor]
    convert_element_type x1 -> x0, other arithmetic: 2.75 us -> none  [shards(): totals = totals.astype(FULL)]
    unnamed x6 -> x0, local copies, waits for them, and re-layouts: 2.13 us -> none
where the time goes in v4:
time: 89.9 us; the launch traced here: 89.7 us
  Pallas kernels  88.9 us (99%)
    pallas_call x1, Pallas kernels, everything(): pl.pallas_call(whole_kernel, out_shape=(jax.ShapeDtypeStruct((2048, 512),...  82.1 us
    pallas_call x1, Pallas kernels, finish(): pl.pallas_call(functools.partial(finish_kernel, factor), out_shape=[jax.S...  6.79 us

profile of v4, /device:TPU:1, one launch (start us, length us, event | category | flops | bytes accessed | tf_op | source)
XLA Modules:
  0.0 89.7 jit_solution(10712211982187206086)
XLA Ops:
  0.6 82.1 %shard_map.196 = (bf16[2048,512]{1,0:T(8,128)(2,1)}, bf16[256,512]{1,0:T(8,128)(2,1)}, bf16[6,512,512]{2,1,0:T(8,128)(2,1)}, f32[8,128]{1,0:T(8,128)}) custom-call(bf16[2048,512]{1,0:T(8,128)(2,1)} %bitcast.5, bf16[256,512]{1,0:T(8,128)(2,1)} %bitcast.7, bf16[2048,512]{1,0:T(8,128)(2,1)} %bitcast.6, s32[12,256]{1,0:T(8,128)} %enc.1, s32[256]{0:T(256)} %counts.1, ...), custom_call_target="tpu_custom_call" | custom-call | tf_op jit(solution)/shard_map/pallas_call | solution.py:531
  82.8 6.8 %shard_map.197 = (bf16[2048,512]{1,0:T(8,128)(2,1)}, bf16[256,512]{1,0:T(8,128)(2,1)}, f32[512,512]{1,0:T(8,128)}, f32[512,512]{1,0:T(8,128)}, f32[512,512]{1,0:...) custom-call(bf16[2048,512]{1,0:T(8,128)(2,1)} %get-tuple-element.22.grid_in, ...), custom_call_target="tpu_custom_call" | custom-call | tf_op jit(solution)/shard_map/pallas_call | solution.py:639

commit v5 on v4

--- a/solution.py
+++ b/solution.py
@@ -50,6 +50,10 @@
     return pl.ds(pl.multiple_of(index * size, size), size)
 
 
+def slope_rows(number, at):
+    return pl.ds(pl.multiple_of(number * DEPTH + at, 16), 16)
+
+
 def half_silu(half_pre):
     bend = jnp.tanh(half_pre)
     lifted = 1.0 + bend
@@ -58,11 +62,11 @@
 
 
 def whole_kernel(
-    grid_any, mesh_any, cot_any, enc, counts, dec,
-    w_recv_any, w_send_any, w_update_any, gain, w_msend_any, w_grecv_any, w_out_any,
+    grid_any, mesh_any, cot_any, enc_any, counts_any, dec_any,
+    w_recv_any, w_send_any, w_update_any, gain_any, w_msend_any, w_grecv_any, w_out_any,
     grid_grad, mesh_grad, totals, gain_total,
     grid_ext, mesh, cot, w_recv, w_send, w_update, w_msend, w_grecv, w_out,
-    stage, enc_col, enc_row, dec_stage, dec_col,
+    enc, counts, dec, gain, stage, enc_col, enc_row, dec_stage, dec_col,
     send_ext, gp, sc, rp, taken, slope, agg, normed, inv, mlat, mesh_ext,
     dcot, dsum, rcot, mc_ext, mesh_rim, lat, mcot, ucot, acot, rsum,
     scot, rim_in, acc, mgrad,
@@ -84,11 +88,15 @@
     for number, (name, source, target) in enumerate((
         ("w_send", w_send_any, w_send),
         ("grid", grid_any, grid_ext.at[pl.ds(GRIM, 2048)]),
+        ("enc", enc_any, enc),
+        ("counts", counts_any, counts),
+        ("dec", dec_any, dec),
         ("mesh", mesh_any, mesh),
         ("w_recv", w_recv_any, w_recv),
         ("w_grecv", w_grecv_any, w_grecv),
         ("cot", cot_any, cot),
         ("w_out", w_out_any, w_out),
+        ("gain", gain_any, gain),
         ("w_update", w_update_any, w_update),
         ("w_msend", w_msend_any, w_msend),
     )):
@@ -114,34 +122,37 @@
         sent.extend(pair)
         return pair
 
+    pl.semaphore_wait(barrier, 12)
+    grid_halo = exchange(
+        0,
+        grid_any.at[pl.ds(0, GRIM)],
+        grid_ext.at[pl.ds(2048 + GRIM, GRIM)],
+        grid_any.at[pl.ds(2048 - GRIM, GRIM)],
+        grid_ext.at[pl.ds(0, GRIM)],
+    )
+
+    def project(start, size):
+        rows = pl.ds(start, size)
+        send_ext[rows] = (dot(grid_ext[rows], w_send[...]) * 0.5).astype(HALF)
+
+    loads["w_send"].wait()
+    loads["grid"].wait()
+    loop(4, lambda step: project(pl.multiple_of(GRIM + step * 512, 256), 512))
+    for name in ("enc", "counts", "dec"):
+        loads[name].wait()
     stage[...] = jnp.zeros_like(stage)
     stage[0:KE] = enc[...] - (place * 2048 - GRIM)
     stage[KE : KE + 1] = counts[...].reshape(1, 256)
     enc_col[...] = jnp.transpose(stage[...])
     for number in range(8):
         for k in range(KE):
-            enc_row[number, :, k * NODES : (k + 1) * NODES] = stage[
+            at = number * DEPTH + k * NODES
+            enc_row[:, at : at + NODES] = stage[
                 k : k + 1, number * NODES : (number + 1) * NODES
             ]
     dec_stage[...] = jnp.zeros_like(dec_stage)
     dec_stage[0:3] = dec[...] - (place * 256 - MRIM)
     dec_col[...] = jnp.transpose(dec_stage[...])
-
-    def project(start, size):
-        rows = pl.ds(start, size)
-        send_ext[rows] = (dot(grid_ext[rows], w_send[...]) * 0.5).astype(HALF)
-
-    loads["w_send"].wait()
-    loads["grid"].wait()
-    loop(4, lambda step: project(pl.multiple_of(GRIM + step * 512, 256), 512))
-    pl.semaphore_wait(barrier, 12)
-    grid_halo = exchange(
-        0,
-        grid_ext.at[pl.ds(GRIM, GRIM)],
-        grid_ext.at[pl.ds(2048 + GRIM, GRIM)],
-        grid_ext.at[pl.ds(2048, GRIM)],
-        grid_ext.at[pl.ds(0, GRIM)],
-    )
 
     loads["mesh"].wait()
     loads["w_recv"].wait()
@@ -180,7 +191,7 @@
                 value, bend = half_silu(taken[at : at + 16] + receiver)
                 mask = jnp.where(number_live > k, 1.0, 0.0)
                 total = total + value * mask
-                slope[number, at : at + 16] = (bend * mask).astype(HALF)
+                slope[slope_rows(number, at)] = (bend * mask).astype(HALF)
             agg[rows] = total.astype(HALF)
 
     loop(7, encode, 1)
@@ -192,6 +203,7 @@
 
     loads["w_update"].wait()
     acot[...] = dot(agg[...], w_update[...])
+    loads["gain"].wait()
     wide_gain = gain[...].astype(FULL).reshape(1, 512)
 
     def normalise(step):
@@ -287,25 +299,44 @@
 
     def everywhere(group):
         own = 2 * group + core
-        copy = remote(
-            terms.at[2 * group + 1 - core], pair_in.at[group], pair_sem.at[group], twin
-        )
-        copy.start()
-        sent.append(copy)
-        yield
-        copy.wait_recv()
-        paired[group] = (terms[own].astype(FULL) + pair_in[group].astype(FULL)).astype(HALF)
+        halves = []
+        for half in range(2):
+            part = pl.ds(256 * half, 256)
+            copy = remote(
+                terms.at[2 * group + 1 - core, :, part],
+                pair_in.at[group, :, part],
+                pair_sem.at[group, half],
+                twin,
+            )
+            copy.start()
+            halves.append(copy)
+            if group == 2 and half == 0:
+                yield
+        sent.extend(halves)
+        yield
         orders = [ORDERS[(p + group) % 3] for p in range(4)]
         columns = [pl.ds(*PARTS[p]) for p in range(4)]
-        waves = [
-            fan(
-                lambda moved: paired.at[group, rows_at(moved, 128), columns[p]],
-                lambda offset: r1.at[group, offset - 1, :, columns[p]],
-                rs_sem.at[4 * group + p],
-                orders[p][0],
-            )
-            for p in range(4)
-        ]
+        waves = []
+        for half in range(2):
+            halves[half].wait_recv()
+            part = pl.ds(256 * half, 256)
+
+            def pair_rows(step):
+                rows = rows_at(step, 64)
+                paired[group, rows, part] = (
+                    terms[own, rows, part].astype(FULL) + pair_in[group, rows, part].astype(FULL)
+                ).astype(HALF)
+
+            loop(8, pair_rows)
+            for p in (2 * half, 2 * half + 1):
+                waves.append(
+                    fan(
+                        lambda moved: paired.at[group, rows_at(moved, 128), columns[p]],
+                        lambda offset: r1.at[group, offset - 1, :, columns[p]],
+                        rs_sem.at[4 * group + p],
+                        orders[p][0],
+                    )
+                )
         yield
         for p in range(4):
             for copy in waves[p]:
@@ -463,23 +494,21 @@
             total = jnp.zeros((16, 512), FULL)
             for k in range(KE):
                 at = k * NODES + part * 16
-                piece = cotangent * slope[number, at : at + 16].astype(FULL)
+                piece = cotangent * slope[slope_rows(number, at)].astype(FULL)
                 total = total + piece
-                slope[number, at : at + 16] = piece.astype(HALF)
+                slope[slope_rows(number, at)] = piece.astype(HALF)
             rsum[rows] = total.astype(HALF)
 
-    def scatter(tile, numbers):
-        total = None
-        for number in numbers:
-            lines = lax.broadcasted_iota(jnp.int32, (256, DEPTH), 0) + tile * 256
-            selector = jnp.where(enc_row[number] == lines, 1.0, 0.0).astype(HALF)
-            piece = dot(selector, slope[number])
-            total = piece if total is None else total + piece
-        scot[rows_at(tile, 256)] = total.astype(HALF)
+    def scatter(tile, first_block, blocks):
+        depth = blocks * DEPTH
+        lines = lax.broadcasted_iota(jnp.int32, (256, depth), 0) + tile * 256
+        rows = pl.ds(pl.multiple_of(first_block * DEPTH, DEPTH), depth)
+        selector = jnp.where(enc_row[:, rows] == lines, 1.0, 0.0).astype(HALF)
+        scot[rows_at(tile, 256)] = dot(selector, slope[rows]).astype(HALF)
 
     loop(2, lambda step: encode_back(step * 7))
-    scatter(0, (0,))
-    scatter(9, (7,))
+    scatter(0, 0, 1)
+    scatter(9, 7, 1)
     grid_back = exchange(
         6,
         scot.at[pl.ds(0, GRIM)],
@@ -488,13 +517,22 @@
         rim_in.at[0],
     )
     loop(7, encode_back, 1)
-    scatter(1, (0, 1))
-    scatter(8, (6, 7))
-    loop(5, lambda tile: scatter(tile, (tile - 2, tile - 1, tile)), 2)
-    loop(8, lambda tile: scatter(tile, (tile - 2, tile - 1, tile)), 5)
+    scatter(1, 0, 2)
+    scatter(8, 6, 2)
+    loop(5, lambda tile: scatter(tile, tile - 2, 3), 2)
+    loop(8, lambda tile: scatter(tile, tile - 2, 3), 5)
     contract(4, mesh, rsum, 1, 256)
-    contract(5, grid_ext, scot, 5, 512)
-    pump(third)
+    for half in range(2):
+        part = pl.ds(256 * half, 256)
+        acc[:, part] = jnp.zeros((512, 256), FULL)
+
+        def send_piece(step):
+            rows = rows_at(step, 512)
+            acc[:, part] += dot(grid_ext[rows], scot[rows, part], ((0,), (0,)))
+
+        loop(5, send_piece)
+        terms[5, :, part] = acc[:, part].astype(HALF)
+        pump(third)
     mgrad[...] = (lat[...] + dot(rsum[...], w_recv[...], ((1,), (1,)))).astype(HALF)
     copy = pltpu.make_async_copy(mgrad, mesh_grad, store_sem.at[3])
     copy.start()
@@ -536,7 +574,7 @@
             jax.ShapeDtypeStruct((6, 512, 512), HALF),
             jax.ShapeDtypeStruct((8, 128), FULL),
         ),
-        in_specs=[anywhere] * 3 + [near] * 3 + [anywhere] * 3 + [near] + [anywhere] * 3,
+        in_specs=[anywhere] * len(operands),
         out_specs=[anywhere, anywhere, anywhere, near],
         scratch_shapes=[
             vmem((2048 + 2 * GRIM, 512), HALF),
@@ -545,9 +583,13 @@
         ]
         + [vmem((512, 512), HALF)] * 6
         + [
+            vmem((KE, 256), jnp.int32),
+            vmem((256,), jnp.int32),
+            vmem((3, 2048), jnp.int32),
+            vmem((512,), HALF),
             vmem((16, 256), jnp.int32),
             vmem((256, 16), jnp.int32),
-            vmem((8, 1, DEPTH), jnp.int32),
+            vmem((1, 8 * DEPTH), jnp.int32),
             vmem((8, 2048), jnp.int32),
             vmem((2048, 8), jnp.int32),
             vmem((2048 + 2 * GRIM, 512), HALF),
@@ -555,7 +597,7 @@
             vmem((2048, 512), FULL),
             vmem((256, 512), FULL),
             vmem((3 * CELLS, 512), FULL),
-            vmem((8, DEPTH, 512), HALF),
+            vmem((8 * DEPTH, 512), HALF),
             vmem((256, 512), HALF),
             vmem((256, 512), FULL),
             vmem((256, 128), FULL),
@@ -585,10 +627,10 @@
             vmem((6, 512, 512), HALF),
             vmem((8, 128), FULL),
             vmem((4, 4, 8, 128), FULL),
-            pltpu.SemaphoreType.DMA((9,)),
+            pltpu.SemaphoreType.DMA((13,)),
             pltpu.SemaphoreType.DMA((5,)),
             pltpu.SemaphoreType.DMA((8, 2)),
-            pltpu.SemaphoreType.DMA((3, 2)),
+            pltpu.SemaphoreType.DMA((3, 2, 2)),
             pltpu.SemaphoreType.DMA((36, 3, 2)),
             pltpu.SemaphoreType.DMA((24, 3, 2)),
             pltpu.SemaphoreType.DMA((3, 4, 2)),
@@ -604,30 +646,36 @@
     grid_out, mesh_out = rest[:2]
     outs = rest[2:8]
     gain_out, held, wide, grid_held, mesh_held, in_sem, out_sem, copy_sem = rest[8:]
-    reads = []
-    for slot in range(6):
-        reads.append(pltpu.make_async_copy(totals.at[slot], held.at[slot], in_sem.at[slot]))
-        reads[slot].start()
     near = [
         pltpu.make_async_copy(grid_in, grid_held, copy_sem.at[0]),
         pltpu.make_async_copy(mesh_in, mesh_held, copy_sem.at[1]),
     ]
-    for copy in near:
+    reads = [
+        pltpu.make_async_copy(totals.at[slot], held.at[slot], in_sem.at[slot])
+        for slot in range(6)
+    ]
+    for copy in reads[:2] + near + reads[2:]:
         copy.start()
     copies = [
         pltpu.make_async_copy(grid_held, grid_out, copy_sem.at[2]),
         pltpu.make_async_copy(mesh_held, mesh_out, copy_sem.at[3]),
     ]
+    for slot in range(6):
+        reads[slot].wait()
+
+        def widen(step):
+            rows = rows_at(step, 64)
+            wide[slot, rows] = held[slot, rows].astype(FULL) * factor
+
+        loop(8, widen)
+        copies.append(pltpu.make_async_copy(wide.at[slot], outs[slot], out_sem.at[slot]))
+        copies[-1].start()
+        if slot == 1:
+            for number in range(2):
+                near[number].wait()
+                copies[number].start()
     for part in range(4):
         gain_out[128 * part : 128 * part + 128] = gain[part] * factor
-    for slot in range(6):
-        reads[slot].wait()
-        wide[slot] = held[slot].astype(FULL) * factor
-        copies.append(pltpu.make_async_copy(wide.at[slot], outs[slot], out_sem.at[slot]))
-        copies[-1].start()
-    for number in range(2):
-        near[number].wait()
-        copies[number].start()
     for copy in copies:
         copy.wait()
 

time: 89.9 us -> 88.8 us (0.988)
  Pallas kernels: 88.9 us -> 87.8 us
    pallas_call x1, Pallas kernels: 82.1 us -> 81.2 us  [everything(): pl.pallas_call(whole_kernel, out_shape=(jax.ShapeDtypeStruct((2048, 512),...]
where the time goes in v5:
time: 88.8 us; the launch traced here: 88.6 us
  Pallas kernels  87.8 us (99%)
    pallas_call x1, Pallas kernels, everything(): pl.pallas_call(whole_kernel, out_shape=(jax.ShapeDtypeStruct((2048, 512),...  81.2 us
    pallas_call x1, Pallas kernels, finish(): pl.pallas_call(functools.partial(finish_kernel, factor), out_shape=[jax.S...  6.65 us

profile of v5, /device:TPU:1, one launch (start us, length us, event | category | flops | bytes accessed | tf_op | source)
XLA Modules:
  0.0 88.6 jit_solution(7093062154176479382)
XLA Ops:
  0.6 81.2 %shard_map.196 = (bf16[2048,512]{1,0:T(8,128)(2,1)}, bf16[256,512]{1,0:T(8,128)(2,1)}, bf16[6,512,512]{2,1,0:T(8,128)(2,1)}, f32[8,128]{1,0:T(8,128)}) custom-call(bf16[2048,512]{1,0:T(8,128)(2,1)} %bitcast.5, bf16[256,512]{1,0:T(8,128)(2,1)} %bitcast.7, bf16[2048,512]{1,0:T(8,128)(2,1)} %bitcast.6, s32[12,256]{1,0:T(8,128)} %enc_any.1, s32[256]{0:T(256)} %counts_any.1, ...), custom_call_target="tpu_custom_call" | custom-call | tf_op jit(solution)/shard_map/pallas_call | solution.py:569
  81.8 6.6 %shard_map.197 = (bf16[2048,512]{1,0:T(8,128)(2,1)}, bf16[256,512]{1,0:T(8,128)(2,1)}, f32[512,512]{1,0:T(8,128)}, f32[512,512]{1,0:T(8,128)}, f32[512,512]{1,0:...) custom-call(bf16[2048,512]{1,0:T(8,128)(2,1)} %get-tuple-element.22.grid_in, ...), custom_call_target="tpu_custom_call" | custom-call | tf_op jit(solution)/shard_map/pallas_call | solution.py:687

commit v6 on v5

--- a/solution.py
+++ b/solution.py
@@ -84,6 +84,13 @@
         moved = lax.rem(coords[axis] + offset, 4)
         return moved, {"graph": place + (moved - coords[axis]) * STRIDES[axis]}
 
+    barrier = pltpu.get_barrier_semaphore()
+    targets = [left, right, twin]
+    targets += [peer(axis, offset)[1] for axis in range(3) for offset in (1, 2, 3)]
+    for target in targets:
+        pl.semaphore_signal(
+            barrier, inc=1, device_id=target, device_id_type=pl.DeviceIdType.MESH
+        )
     loads = {}
     for number, (name, source, target) in enumerate((
         ("w_send", w_send_any, w_send),
@@ -103,13 +110,6 @@
         loads[name] = pltpu.make_async_copy(source, target, load_sem.at[number])
         loads[name].start()
 
-    barrier = pltpu.get_barrier_semaphore()
-    targets = [left, right, twin]
-    targets += [peer(axis, offset)[1] for axis in range(3) for offset in (1, 2, 3)]
-    for target in targets:
-        pl.semaphore_signal(
-            barrier, inc=1, device_id=target, device_id_type=pl.DeviceIdType.MESH
-        )
     sent = []
 
     def exchange(index, low, low_target, high, high_target):
@@ -242,15 +242,14 @@
             rows = pl.ds(pl.multiple_of(number * CELLS + step * 16, 16), 16)
             own = gp[rows]
             cotangent = sc[rows]
-            total = jnp.zeros((16, 512), FULL)
-            back = jnp.zeros((16, 512), FULL)
+            total = back = None
             for j in range(3):
                 value, bend = half_silu(
                     taken[pl.ds(pl.multiple_of(j * CELLS + step * 16, 16), 16)] + own
                 )
-                total = total + value
                 part = cotangent * bend
-                back = back + part
+                total = value if j == 0 else total + value
+                back = part if j == 0 else back + part
                 dcot[j, inner] = part.astype(HALF)
             dsum[rows] = total.astype(HALF)
             rcot[rows] = back.astype(HALF)

time: 88.8 us -> 88.8 us (level)
  no operation moved by 1% of the time
where the time goes in v6:
time: 88.8 us; the launch traced here: 88.7 us
  Pallas kernels  87.9 us (99%)
    pallas_call x1, Pallas kernels, everything(): pl.pallas_call(whole_kernel, out_shape=(jax.ShapeDtypeStruct((2048, 512),...  81.2 us
    pallas_call x1, Pallas kernels, finish(): pl.pallas_call(functools.partial(finish_kernel, factor), out_shape=[jax.S...  6.65 us

profile of v6, /device:TPU:1, one launch (start us, length us, event | category | flops | bytes accessed | tf_op | source)
XLA Modules:
  0.0 88.7 jit_solution(15125301672595786797)
XLA Ops:
  0.6 81.2 %shard_map.196 = (bf16[2048,512]{1,0:T(8,128)(2,1)}, bf16[256,512]{1,0:T(8,128)(2,1)}, bf16[6,512,512]{2,1,0:T(8,128)(2,1)}, f32[8,128]{1,0:T(8,128)}) custom-call(bf16[2048,512]{1,0:T(8,128)(2,1)} %bitcast.5, bf16[256,512]{1,0:T(8,128)(2,1)} %bitcast.7, bf16[2048,512]{1,0:T(8,128)(2,1)} %bitcast.6, s32[12,256]{1,0:T(8,128)} %enc_any.1, s32[256]{0:T(256)} %counts_any.1, ...), custom_call_target="tpu_custom_call" | custom-call | tf_op jit(solution)/shard_map/pallas_call | solution.py:568
  81.9 6.6 %shard_map.197 = (bf16[2048,512]{1,0:T(8,128)(2,1)}, bf16[256,512]{1,0:T(8,128)(2,1)}, f32[512,512]{1,0:T(8,128)}, f32[512,512]{1,0:T(8,128)}, f32[512,512]{1,0:...) custom-call(bf16[2048,512]{1,0:T(8,128)(2,1)} %get-tuple-element.22.grid_in, ...), custom_call_target="tpu_custom_call" | custom-call | tf_op jit(solution)/shard_map/pallas_call | solution.py:686
